TPU v7x, 256 devices: a whole 4x4x8 slice. The times are simulated.
256 devices in a mesh: section: 2 (over core), dp: 8 (over x, y_lo), tensor: 16 (over z, y_hi).
Axes of the slice: x: 4, y: 4 (y_hi: 2, y_lo: 2; y = y_hi * 2 + y_lo), z: 8, core: 2. Of those that a mesh axis runs over, the one named last changes fastest.
Arguments:
- layer_inputs: bfloat16 [2, 1024, 9216], P('section', 'tensor', 'dp'), may hold values from -0.75 to 0.75
- projection: bfloat16 [2, 9216, 36864], P('section', 'dp', 'tensor'), may hold values from -0.0625 to 0.0625
- pre_act: bfloat16 [2, 1024, 36864], P('section', 'dp', 'tensor'), may hold values from -6 to 6
- act_grad: bfloat16 [2, 1024, 36864], P('section', 'dp', 'tensor'), may hold values from -2 to 2
Outputs:
- weight_grad: bfloat16 [2, 9216, 36864], P('section', 'dp', 'tensor')
- prev_grad: bfloat16 [2, 1024, 9216], P('section', 'tensor', 'dp')
All inputs are finite; a program needn't handle non-finite values.
Results may differ from a plain program's by a relative error of at most 0.019.
Values may be sent and summed in bfloat16 or wider, within the bound.
No kernel may reach another device: no remote copies, remote signals or barrier semaphores. Data moves between devices by JAX's collectives and lax.ppermute only.
A program may use at most 64 MiB of HBM per device.

v0:
```python
import jax
import jax.numpy as jnp
from jax import lax
from jax.sharding import PartitionSpec as P


def passed_along(block, axis, distance):
    devices = range(lax.axis_size(axis))
    route = [((i - distance) % len(devices), i) for i in devices]
    return lax.ppermute(block, axis, route)


def on_device(layer_inputs, projection, pre_act, act_grad):
    inputs = layer_inputs[0]
    weight = projection[0]
    pre_grad = (
        2.0 * jnp.maximum(pre_act[0].astype(jnp.float32), 0.0) * act_grad[0].astype(jnp.float32)
    ).astype(jnp.bfloat16)
    all_inputs = lax.all_gather(inputs, "tensor", axis=0, tiled=True)
    all_grads = lax.all_gather(pre_grad, "dp", axis=0, tiled=True)
    accum = lax.dot_general(
        all_inputs, all_grads, (((0,), (0,)), ((), ())), preferred_element_type=jnp.float32
    )
    weight_grad = accum.astype(jnp.bfloat16)
    summed = lax.psum_scatter(
        lax.dot_general(
            all_grads, weight, (((1,), (1,)), ((), ())), preferred_element_type=jnp.float32
        ).astype(jnp.bfloat16),
        "tensor",
        scatter_dimension=0,
        tiled=True,
    )
    handed = passed_along(summed, "section", -1)
    return (weight_grad[None], handed[None])


def solution(mesh):
    return jax.shard_map(
        on_device,
        mesh=mesh,
        in_specs=(
            P("section", "tensor", "dp"),
            P("section", "dp", "tensor"),
            P("section", "dp", "tensor"),
            P("section", "dp", "tensor"),
        ),
        out_specs=(P("section", "dp", "tensor"), P("section", "tensor", "dp")),
        check_vma=False,
    )
```

profile of v0, /device:TPU:1, one launch (start us, length us, event | category | flops | bytes accessed | tf_op | source)
XLA Modules:
  0.0 450.2 jit_solution(8120152749903391107)
XLA Ops:
  7.2 0.0 all-gather.5.cloned.1.call-start
  7.2 2.3 multiply_convert_fusion
  9.5 0.0 all-gather.5.cloned.1.call-update
  9.5 0.0 reduce-scatter.2.cloned.1.call-start
  9.6 106.7 %all-gather.5.cloned.1.call-done = bf16[1,1024,2304]{2,1,0:T(8,128)(2,1)} async-done(((bf16[1,128,2304]{2,1,0:T(8,128)(2,1)}), bf16[1,1024,2304]{2,1,0:T(8,128)(2,1)}) %all-gather.5.cloned.1.call-update) | async-done | bytes 4718608 | tf_op jit(solution)/shard_map/all_gather | solution.py:20
  116.3 10.7 %fusion.5 = bf16[1024,1152]{1,0:T(8,128)(2,1)} fusion(bf16[1,1152,2304]{2,1,0:T(8,128)(2,1)} %param.5, bf16[1,1024,2304]{2,1,0:T(8,128)(2,1)} %all-gather.5.cloned.1.call-done), kind=kOutput, calls=%fused_computation.6 | convolution fusion | flops 5436997632 | bytes 12386304 | tf_op jit(solution)/shard_map/dot_general | solution.py:26
  127.0 0.0 reduce-scatter.2.cloned.1.call-update
  127.0 0.0 all-gather.7.cloned.1.call-start
  127.1 0.7 all-gather.7.cloned.1.call-update
  127.8 207.8 %reduce-scatter.2.cloned.1.call-done = bf16[64,1152]{1,0:T(8,128)(2,1)} async-done(((bf16[1024,1152]{1,0:T(8,128)(2,1)}), bf16[64,1152]{1,0:T(8,128)(2,1)}) %reduce-scatter.2.cloned.1.call-update) | async-done | bytes 147472 | tf_op jit(solution)/shard_map/reduce_scatter | solution.py:25
  335.6 4.7 %collective-permute-start = (bf16[64,1152]{1,0:T(8,128)(2,1)}, bf16[64,1152]{1,0:T(8,128)(2,1)S(1)}, u32[]{:S(2)}, u32[]{:S(2)}) collective-permute-start(bf16[64,1152]{1,0:T(8,128)(2,1)} %reduce-scatter.2.cloned.1.call-done), channel_id=1, source_target_pairs={{128,0},{0,128},{129,1},{1,129},{130,2},{2,130},{131,3},{3,131},{1... | collective-permute-start | bytes 442376 | tf_op jit(solution)/shard_map/ppermute | solution.py:10
  340.3 83.8 %all-gather.7.cloned.1.call-done = bf16[1,1024,1152]{2,1,0:T(8,128)(2,1)} async-done(((bf16[1,64,1152]{2,1,0:T(8,128)(2,1)}), bf16[1,1024,1152]{2,1,0:T(8,128)(2,1)}) %all-gather.7.cloned.1.call-update) | async-done | bytes 2359312 | tf_op jit(solution)/shard_map/all_gather | solution.py:19
  424.0 10.4 %fusion = bf16[1,1152,2304]{1,2,0:T(8,128)(2,1)} fusion(bf16[1,1024,2304]{2,1,0:T(8,128)(2,1)} %all-gather.5.cloned.1.call-done, bf16[1,1024,1152]{2,1,0:T(8,128)(2,1)} %all-gather.7.cloned.1.call-done), kind=kOutput, calls=%fused_computation.1 | convolution fusion | flops 5438472192 | bytes 12386304 | tf_op jit(solution)/shard_map/dot_general | solution.py:21
  434.5 8.5 %copy.6 = bf16[1,1152,2304]{2,1,0:T(8,128)(2,1)} copy(bf16[1,1152,2304]{1,2,0:T(8,128)(2,1)} %fusion) | data formatting | bytes 10616832
  443.0 0.0 collective-permute-done
  443.0 0.7 copy.8
Async XLA Ops:
  7.2 109.1 %all-gather.5.cloned.1.call-start = ((), (), s32[]{:S(2)}) async-start(), calls=%async_computation.2 | async-start | bytes 5308416 | tf_op jit(solution)/shard_map/all_gather | solution.py:20
  9.5 326.1 %reduce-scatter.2.cloned.1.call-start = ((), (), s32[]{:S(2)}) async-start(), calls=%async_computation.1 | async-start | bytes 2506752 | tf_op jit(solution)/shard_map/reduce_scatter | solution.py:25
  127.0 297.0 %all-gather.7.cloned.1.call-start = ((), (), s32[]{:S(2)}) async-start(), calls=%async_computation.3 | async-start | bytes 2506752 | tf_op jit(solution)/shard_map/all_gather | solution.py:19
  335.6 107.4 %collective-permute-start = (bf16[64,1152]{1,0:T(8,128)(2,1)}, bf16[64,1152]{1,0:T(8,128)(2,1)S(1)}, u32[]{:S(2)}, u32[]{:S(2)}) collective-permute-start(bf16[64,1152]{1,0:T(8,128)(2,1)} %reduce-scatter.2.cloned.1.call-done), channel_id=1, source_target_pairs={{128,0},{0,128},{129,1},{1,129},{130,2},{2,130},{131,3},{3,131},{1... | collective-permute-start | bytes 442376 | tf_op jit(solution)/shard_map/ppermute | solution.py:10
Sparse Core Ops, SparseCore 0:
  10.4 105.8 all-gather.4
  127.1 208.3 reduce-scatter.1
  338.2 85.8 all-gather.6
where the time goes:
time: 453 us; the launch traced here: 450 us
  waiting for transfers between devices  399 us (88%)
  matrix products  21.2 us (5%)
  between operations  13.7 us (3%)
  local copies, waits for them, and re-layouts  9.2 us (2%)
  starting transfers between devices  4.81 us (1%)
    reduce_scatter x1, waiting for transfers between devices, on_device(): lax.psum_scatter(lax.dot_general(all_grads, weight, (((1,), (1,)), ((), (...  208 us
    all_gather x1, waiting for transfers between devices, on_device(): all_grads = lax.all_gather(pre_grad, 'dp', axis=0, tiled=True)  107 us
    all_gather x1, waiting for transfers between devices, on_device(): all_inputs = lax.all_gather(inputs, 'tensor', axis=0, tiled=True)  83.8 us
    dot_general x1, matrix products, on_device(): lax.dot_general(all_grads, weight, (((1,), (1,)), ((), ())), preferred_el...  10.7 us
    dot_general x1, matrix products, on_device(): lax.dot_general(all_inputs, all_grads, (((0,), (0,)), ((), ())), preferre...  10.4 us
    unnamed x2, local copies, waits for them, and re-layouts  9.2 us
  transfers between devices with their start and end apart: 4, of which 3 were waited for; matrix products, arithmetic and copies ran while one was open for 4% of the time, Pallas kernels for 0%

commit v1 on v0

v1 whole, which is shorter than its diff:
```python
import jax
import jax.numpy as jnp
from jax import lax
from jax.sharding import PartitionSpec as P

F32, BF16 = jnp.float32, jnp.bfloat16


def shift(block, axis, distance):
    n = lax.axis_size(axis)
    return lax.ppermute(block, axis, [(i, (i + distance) % n) for i in range(n)])


def swap(block, axis):
    n = lax.axis_size(axis)
    return lax.ppermute(block, axis, [(i, i ^ 1) for i in range(n)])


def gather_inputs(own, z_size, y_hi):
    other = swap(own, "tensor")
    pair = jnp.where(y_hi == 0, jnp.concatenate([own, other]), jnp.concatenate([other, own]))
    half = own.shape[0]
    got = {0: pair}
    up, down = pair, pair
    for step in range(1, z_size // 2):
        up = shift(up, "tensor", 2)
        down = shift(down, "tensor", -2)
        got[z_size - step] = up
        got[step] = down
    far_up = shift(up[:half], "tensor", 2)
    far_down = shift(down[half:], "tensor", -2)
    got[z_size // 2] = jnp.concatenate([far_up, far_down])
    return jnp.concatenate([got[i] for i in range(z_size)])


def on_device(layer_inputs, projection, pre_act, act_grad):
    weight = projection[0]
    dp, tensor = lax.axis_index("dp"), lax.axis_index("tensor")
    x, y_lo, z, y_hi = dp // 2, dp % 2, tensor // 2, tensor % 2
    rows = pre_act.shape[1]
    half = rows // 2
    wide = pre_act.shape[2]
    third = wide // 3

    own = (
        2.0 * jnp.maximum(pre_act[0].astype(F32), 0.0) * act_grad[0].astype(F32)
    ).astype(BF16)

    inputs = gather_inputs(layer_inputs[0], 8, y_hi)

    left = shift(own, "dp", 2)
    right = shift(own, "dp", -2)
    beside = swap(own, "dp")
    from_left = shift(jnp.concatenate([left[:half], beside[:half]]), "dp", 2)
    from_right = shift(jnp.concatenate([right[half:], beside[:half]]), "dp", -2)
    from_beside = swap(jnp.concatenate([left[half:], right[half:]]), "dp")
    across = jnp.concatenate([from_left[:half], from_right[:half]])
    left_beside = jnp.concatenate([from_left[half:], from_beside[:half]])
    right_beside = jnp.concatenate([from_right[half:], from_beside[half:]])
    far = jnp.concatenate(
        [
            shift(left_beside[:, :third], "dp", 2),
            shift(right_beside[:, third : 2 * third], "dp", -2),
            swap(across[:, 2 * third :], "dp"),
        ],
        axis=1,
    )
    order = [
        ((0, 0), own),
        ((0, 1), beside),
        ((1, 0), right),
        ((3, 0), left),
        ((1, 1), right_beside),
        ((2, 0), across),
        ((3, 1), left_beside),
        ((2, 1), far),
    ]
    partial = jnp.zeros((8 * rows, weight.shape[0]), BF16)
    places = []
    for (dx, dy), block in order:
        place = ((x + dx) % 4) * 2 + (y_lo ^ dy)
        places.append(place)
        part = lax.dot_general(block, weight, (((1,), (1,)), ((), ())), preferred_element_type=F32)
        partial = lax.dynamic_update_slice(partial, part.astype(BF16), (place * rows, 0))

    def part_of(offset, start=0, size=rows):
        where = ((z + offset) % 8) * rows + start
        return lax.dynamic_slice(partial, (where, 0), (size, partial.shape[1])).astype(F32)

    up = shift(part_of(4, 0, half).astype(BF16), "tensor", 2)
    down = shift(part_of(4, half, half).astype(BF16), "tensor", -2)
    up = jnp.concatenate([part_of(3, 0, half) + up.astype(F32), part_of(3, half, half)])
    down = jnp.concatenate([part_of(-3, 0, half), part_of(-3, half, half) + down.astype(F32)])
    up = shift(up.astype(BF16), "tensor", 2)
    down = shift(down.astype(BF16), "tensor", -2)
    for offset in (2, 1):
        up = shift((part_of(offset) + up.astype(F32)).astype(BF16), "tensor", 2)
        down = shift((part_of(-offset) + down.astype(F32)).astype(BF16), "tensor", -2)
    total = part_of(0) + up.astype(F32) + down.astype(F32)
    mine = lax.dynamic_slice(total, (y_hi * half, 0), (half, total.shape[1])).astype(BF16)
    theirs = lax.dynamic_slice(total, ((1 - y_hi) * half, 0), (half, total.shape[1])).astype(BF16)
    near = lax.ppermute(mine, "section", [(0, 1), (1, 0)])
    across_pair = [
        (s * 16 + t, (1 - s) * 16 + (t ^ 1)) for s in range(2) for t in range(16)
    ]
    away = lax.ppermute(theirs, ("section", "tensor"), across_pair)
    handed = (near.astype(F32) + away.astype(F32)).astype(BF16)

    grads = jnp.concatenate([block for _, block in order])
    matched = jnp.concatenate(
        [
            lax.dynamic_slice(inputs, (((place - z) % 8) * rows, 0), (rows, inputs.shape[1]))
            for place in places
        ]
    )
    weight_grad = lax.dot_general(
        matched, grads, (((0,), (0,)), ((), ())), preferred_element_type=F32
    ).astype(BF16)
    return (weight_grad[None], handed[None])


def solution(mesh):
    return jax.shard_map(
        on_device,
        mesh=mesh,
        in_specs=(
            P("section", "tensor", "dp"),
            P("section", "dp", "tensor"),
            P("section", "dp", "tensor"),
            P("section", "dp", "tensor"),
        ),
        out_specs=(P("section", "dp", "tensor"), P("section", "tensor", "dp")),
        check_vma=False,
    )
```

time: 453 us -> 118 us (0.26)
  waiting for transfers between devices: 399 us -> 33.7 us
  starting transfers between devices: 4.81 us -> 53.3 us
  between operations: 13.7 us -> 1.2 us
  local copies, waits for them, and re-layouts: 9.2 us -> 1.33 us
    reduce_scatter x1 -> x0, waiting for transfers between devices: 208 us -> none  [on_device(): lax.psum_scatter(lax.dot_general(all_grads, weight, (((1,), (1,)), ((), (...]
    all_gather x2 -> x0, waiting for transfers between devices: 190 us -> none  [the longest x1 107 us: on_device(): all_grads = lax.all_gather(pre_grad, 'dp', axis=0, tiled=True)]
    ppermute x1 -> x28, starting transfers between devices: 4.69 us -> 53.3 us  [the longest x22 32.9 us: shift(): lax.ppermute(block, axis, [(i, (i + distance) % n) for i in range(n)])]
    ppermute x1 -> x28, waiting for transfers between devices: 0.01 us -> 33.7 us  [the longest x22 33.7 us: shift(): lax.ppermute(block, axis, [(i, (i + distance) % n) for i in range(n)])]
    unnamed x2 -> x32, local copies, waits for them, and re-layouts: 9.2 us -> 0.69 us
    dot_general x2 -> x9, matrix products: 21.2 us -> 24.4 us  [the longest x8 16.9 us: on_device(): lax.dot_general(block, weight, (((1,), (1,)), ((), ())), preferred_elemen...]
  transfers between devices with their start and end apart: 4 -> 28, of which waited for: 3 -> 9; matrix products, arithmetic and copies ran while one was open for 4% -> 23% of each run, Pallas kernels for 0% -> 0%
where the time goes in v1:
time: 118 us
  starting transfers between devices  53.3 us (45%)
  waiting for transfers between devices  33.7 us (29%)
  matrix products  24.4 us (21%)
  other arithmetic  3.75 us (3%)
  local copies, waits for them, and re-layouts  1.33 us (1%)
  between operations  1.2 us (1%)
    ppermute x22, waiting for transfers between devices, shift(): lax.ppermute(block, axis, [(i, (i + distance) % n) for i in range(n)])  33.7 us
    ppermute x22, starting transfers between devices, shift(): lax.ppermute(block, axis, [(i, (i + distance) % n) for i in range(n)])  32.9 us
    dot_general x8, matrix products, on_device(): lax.dot_general(block, weight, (((1,), (1,)), ((), ())), preferred_elemen...  16.9 us
    ppermute x1, starting transfers between devices, on_device(): near = lax.ppermute(mine, 'section', [(0, 1), (1, 0)])  13.1 us
    dot_general x1, matrix products, on_device(): lax.dot_general(matched, grads, (((0,), (0,)), ((), ())), preferred_eleme...  7.43 us
    ppermute x4, starting transfers between devices, swap(): return lax.ppermute(block, axis, [(i, i ^ 1) for i in range(n)])  5.78 us
  transfers between devices with their start and end apart: 28, of which 9 were waited for; matrix products, arithmetic and copies ran while one was open for 23% of the time, Pallas kernels for 0%

profile of v1, /device:TPU:1, one launch (start us, length us, event | category | flops | bytes accessed | tf_op | source)
XLA Modules:
  0.0 117.6 jit_solution(14390991403471557135)
XLA Ops:
  0.6 3.8 %collective-permute-start = (bf16[64,1152]{1,0:T(8,128)(2,1)}, bf16[64,1152]{1,0:T(8,128)(2,1)S(1)}, u32[]{:S(2)}, u32[]{:S(2)}) collective-permute-start(bf16[64,1152]{1,0:T(8,128)(2,1)} %bitcast.65), channel_id=1, source_target_pairs={{0,1},{1,0},{2,3},{3,2},{4,5},{5,4},{6,7},{7,6},{8,9},{9,8},{10,11... | collective-permute-start | bytes 442376 | tf_op jit(solution)/shard_map/ppermute | solution.py:16
  4.5 2.3 %constant_dynamic-update-slice_fusion.19 = (bf16[1024,2304]{1,0:T(8,128)(2,1)}, bf16[128,2304]{1,0:T(8,128)(2,1)S(1)}) fusion(bf16[1,128,2304]{2,1,0:T(8,128)(2,1)} %param.7, bf16[1,128,2304]{2,1,0:T(8,128)(2,1)} %param.6), kind=kLoop, calls=%fused_computation.97 | loop fusion | flops 1769471 | bytes 2359296
  6.7 0.4 collective-permute-start.9
  7.1 2.5 %collective-permute-start.10 = (bf16[128,2304]{1,0:T(8,128)(2,1)S(1)}, bf16[128,2304]{1,0:T(8,128)(2,1)S(1)}, u32[]{:S(2)}, u32[]{:S(2)}) collective-permute-start(bf16[128,2304]{1,0:T(8,128)(2,1)S(1)} %get-tuple-element.3), channel_id=1, source_target_pairs={{0,96},{16,112},{32,0},{48,16},{64,32},{80,48},{96,64},{112,80},{1... | collective-permute-start | bytes 1769480 | tf_op jit(solution)/shard_map/ppermute | solution.py:11
  9.7 5.7 %collective-permute-start.1 = (bf16[128,1152]{1,0:T(8,128)(2,1)S(1)}, bf16[128,1152]{1,0:T(8,128)(2,1)S(1)}, u32[]{:S(2)}, u32[]{:S(2)}) collective-permute-start(bf16[128,1152]{1,0:T(8,128)(2,1)S(1)} %get-tuple-element.5), channel_id=1, source_target_pairs={{0,14},{1,15},{2,0},{3,1},{4,2},{5,3},{6,4},{7,5},{8,6},{9,7},{10,... | collective-permute-start | bytes 884744 | tf_op jit(solution)/shard_map/ppermute | solution.py:11
  15.4 0.2 broadcast_in_dim.10
  15.6 4.4 %fusion.62 = bf16[1024,1152]{1,0:T(8,128)(2,1)S(1)} fusion(bf16[1024,1152]{1,0:T(8,128)(2,1)S(1)} %broadcast_in_dim.10, s32[]{:T(128)S(6)} %select_n.233, bf16[128,2304]{1,0:T(8,128)(2,1)S(1)} %get-tuple-element.3, bf16[1,1152,2304]{2,1,0:T(8,128)(2,1)} %param.5), kind=kOutput, calls=%fused_computation.33 | convolution fusion | flops 679624704 | bytes 6193156 | tf_op jit(solution)/shard_map/dot_general | solution.py:83
  20.0 0.1 collective-permute-done.1
  20.1 3.4 %collective-permute-start.2 = (bf16[128,1152]{1,0:T(8,128)(2,1)S(1)}, bf16[128,1152]{1,0:T(8,128)(2,1)S(1)}, u32[]{:S(2)}, u32[]{:S(2)}) collective-permute-start(bf16[128,1152]{1,0:T(8,128)(2,1)S(1)} %collective-permute-done.1), channel_id=1, source_target_pairs={{0,14},{1,15},{2,0},{3,1},{4,2},{5,3},{6,4},{7,5},{8,6},{9,7},{10,... | collective-permute-start | bytes 884744 | tf_op jit(solution)/shard_map/ppermute | solution.py:11
  23.6 0.5 collective-permute-done.11
  24.2 0.1 pad_maximum_fusion
  24.3 2.0 %collective-permute-start.12 = (bf16[128,2304]{1,0:T(8,128)(2,1)S(1)}, bf16[128,2304]{1,0:T(8,128)(2,1)S(1)}, u32[]{:S(2)}, u32[]{:S(2)}) collective-permute-start(bf16[128,2304]{1,0:T(8,128)(2,1)S(1)} %get-tuple-element.28), channel_id=1, source_target_pairs={{0,96},{16,112},{32,0},{48,16},{64,32},{80,48},{96,64},{112,80},{1... | collective-permute-start | bytes 1769480 | tf_op jit(solution)/shard_map/ppermute | solution.py:11
  26.3 1.1 collective-permute-start.13
  27.5 1.8 %fusion.59 = bf16[1024,1152]{1,0:T(8,128)(2,1)S(1)} fusion(bf16[1024,1152]{1,0:T(8,128)(2,1)S(1)} %fusion.62, s32[]{:T(128)S(6)} %select_n.234, bf16[128,2304]{1,0:T(8,128)(2,1)S(1)} %collective-permute-done.9, bf16[1,1152,2304]{2,1,0:T(8,128)(2,1)S(1)} %bitcast.64), kind=kOutput, calls=%fused_computation.32 | convolution fusion | flops 679624704 | bytes 6193156 | tf_op jit(solution)/shard_map/dot_general | solution.py:83
  29.3 1.8 %fusion.56 = bf16[1024,1152]{1,0:T(8,128)(2,1)S(1)} fusion(bf16[1024,1152]{1,0:T(8,128)(2,1)S(1)} %fusion.59, s32[]{:T(128)S(6)} %select_n.235, bf16[128,2304]{1,0:T(8,128)(2,1)S(1)} %collective-permute-done.10, bf16[1,1152,2304]{2,1,0:T(8,128)(2,1)S(1)} %bitcast.64), kind=kOutput, calls=%fused_computation.31 | convolution fusion | flops 679624704 | bytes 6193156 | tf_op jit(solution)/shard_map/dot_general | solution.py:83
  31.1 1.8 %fusion.53 = bf16[1024,1152]{1,0:T(8,128)(2,1)S(1)} fusion(bf16[1024,1152]{1,0:T(8,128)(2,1)S(1)} %fusion.56, s32[]{:T(128)S(6)} %select_n.236, bf16[128,2304]{1,0:T(8,128)(2,1)S(1)} %collective-permute-done.11, bf16[1,1152,2304]{2,1,0:T(8,128)(2,1)S(1)} %bitcast.64), kind=kOutput, calls=%fused_computation.30 | convolution fusion | flops 679624704 | bytes 6193156 | tf_op jit(solution)/shard_map/dot_general | solution.py:83
  32.9 5.2 %collective-permute-start.3 = (bf16[128,1152]{1,0:T(8,128)(2,1)S(1)}, bf16[128,1152]{1,0:T(8,128)(2,1)S(1)}, u32[]{:S(2)}, u32[]{:S(2)}) collective-permute-start(bf16[128,1152]{1,0:T(8,128)(2,1)S(1)} %collective-permute-done.2), channel_id=1, source_target_pairs={{0,14},{1,15},{2,0},{3,1},{4,2},{5,3},{6,4},{7,5},{8,6},{9,7},{10,... | collective-permute-start | bytes 884744 | tf_op jit(solution)/shard_map/ppermute | solution.py:11
  38.2 6.7 %collective-permute-done.6 = bf16[128,1152]{1,0:T(8,128)(2,1)S(1)} collective-permute-done((bf16[128,1152]{1,0:T(8,128)(2,1)S(1)}, bf16[128,1152]{1,0:T(8,128)(2,1)S(1)}, u32[]{:S(2)}, u32[]{:S(2)}) %collective-permute-start.6) | collective-permute-done | bytes 294944 | tf_op jit(solution)/shard_map/ppermute | solution.py:11
  44.9 0.1 collective-permute-start.7
  45.0 2.7 %collective-permute-start.8 = (bf16[64,1152]{1,0:T(8,128)(2,1)S(1)}, bf16[64,1152]{1,0:T(8,128)(2,1)S(1)}, u32[]{:S(2)}, u32[]{:S(2)}) collective-permute-start(bf16[64,1152]{1,0:T(8,128)(2,1)S(1)} %slice.63), channel_id=1, source_target_pairs={{0,14},{1,15},{2,0},{3,1},{4,2},{5,3},{6,4},{7,5},{8,6},{9,7},{10,... | collective-permute-start | bytes 442376 | tf_op jit(solution)/shard_map/ppermute | solution.py:11
  48.1 0.1 collective-permute-start.15
  48.2 0.5 collective-permute-start.17
  48.7 3.0 %collective-permute-start.16 = (bf16[128,768]{1,0:T(8,128)(2,1)S(1)}, bf16[128,768]{1,0:T(8,128)(2,1)S(1)}, u32[]{:S(2)}, u32[]{:S(2)}) collective-permute-start(bf16[128,768]{1,0:T(8,128)(2,1)S(1)} %pad_maximum_fusion.6), channel_id=1, source_target_pairs={{0,96},{16,112},{32,0},{48,16},{64,32},{80,48},{96,64},{112,80},{1... | collective-permute-start | bytes 589832 | tf_op jit(solution)/shard_map/ppermute | solution.py:11
  51.6 1.8 %fusion.50 = bf16[1024,1152]{1,0:T(8,128)(2,1)S(1)} fusion(bf16[1024,1152]{1,0:T(8,128)(2,1)S(1)} %fusion.53, s32[]{:T(128)S(6)} %select_n.237, bf16[1,1152,2304]{2,1,0:T(8,128)(2,1)S(1)} %bitcast.64, bf16[64,2304]{1,0:T(8,128)(2,1)S(1)} %get-tuple-element.20, bf16[64,2304]{1,0:T(8,128)(2,1)S(1)} %get-tuple-element.19), kind=kOutput, calls=%fused_computation.29 | convolution fusion | flops 680804352 | bytes 6193156 | tf_op jit(solution)/shard_map/dot_general | solution.py:83
  53.4 1.8 %fusion.47 = bf16[1024,1152]{1,0:T(8,128)(2,1)S(1)} fusion(bf16[1024,1152]{1,0:T(8,128)(2,1)S(1)} %fusion.50, s32[]{:T(128)S(6)} %select_n.238, bf16[1,1152,2304]{2,1,0:T(8,128)(2,1)S(1)} %bitcast.64, bf16[64,2304]{1,0:T(8,128)(2,1)S(1)} %get-tuple-element.17, bf16[64,2304]{1,0:T(8,128)(2,1)S(1)} %get-tuple-element.14), kind=kOutput, calls=%fused_computation.28 | convolution fusion | flops 680804352 | bytes 6193156 | tf_op jit(solution)/shard_map/dot_general | solution.py:83
  55.2 1.8 %fusion.44 = bf16[1024,1152]{1,0:T(8,128)(2,1)S(1)} fusion(bf16[1024,1152]{1,0:T(8,128)(2,1)S(1)} %fusion.47, s32[]{:T(128)S(6)} %select_n.239, bf16[1,1152,2304]{2,1,0:T(8,128)(2,1)S(1)} %bitcast.64, bf16[64,2304]{1,0:T(8,128)(2,1)S(1)} %get-tuple-element.22, bf16[64,2304]{1,0:T(8,128)(2,1)S(1)} %get-tuple-element.16), kind=kOutput, calls=%fused_computation.27 | convolution fusion | flops 680804352 | bytes 6193156 | tf_op jit(solution)/shard_map/dot_general | solution.py:83
  57.4 1.8 %fusion.41 = bf16[1024,1152]{1,0:T(8,128)(2,1)S(1)} fusion(bf16[1024,1152]{1,0:T(8,128)(2,1)S(1)} %fusion.44, s32[]{:T(128)S(6)} %select_n.240, bf16[1,1152,2304]{2,1,0:T(8,128)(2,1)S(1)} %bitcast.64, bf16[128,768]{1,0:T(8,128)(2,1)S(1)} %collective-permute-done.17, bf16[128,768]{1,0:T(8,128)(2,1)S(1)} %collective-permute-done.16, ...), kind=kOutput, calls=%fused_computation.26 | convolution fusion | flops 681394176 | bytes 6193156 | tf_op jit(solution)/shard_map/dot_general | solution.py:83
  59.3 0.1 collective-permute-start.18
  59.4 2.7 %collective-permute-start.22 = (bf16[64,1152]{1,0:T(8,128)(2,1)S(1)}, bf16[64,1152]{1,0:T(8,128)(2,1)S(1)}, u32[]{:S(2)}, u32[]{:S(2)}) collective-permute-start(bf16[64,1152]{1,0:T(8,128)(2,1)S(1)} %get-tuple-element.11), channel_id=1, source_target_pairs={{0,14},{1,15},{2,0},{3,1},{4,2},{5,3},{6,4},{7,5},{8,6},{9,7},{10,... | collective-permute-start | bytes 442376 | tf_op jit(solution)/shard_map/ppermute | solution.py:11
  62.0 2.5 %collective-permute-done.18 = bf16[64,1152]{1,0:T(8,128)(2,1)S(1)} collective-permute-done((bf16[64,1152]{1,0:T(8,128)(2,1)S(1)}, bf16[64,1152]{1,0:T(8,128)(2,1)S(1)}, u32[]{:S(2)}, u32[]{:S(2)}) %collective-permute-start.18) | collective-permute-done | bytes 147488 | tf_op jit(solution)/shard_map/ppermute | solution.py:11
  64.7 0.1 collective-permute-start.19
  64.8 2.7 %collective-permute-start.23 = (bf16[128,1152]{1,0:T(8,128)(2,1)S(1)}, bf16[128,1152]{1,0:T(8,128)(2,1)S(1)}, u32[]{:S(2)}, u32[]{:S(2)}) collective-permute-start(bf16[128,1152]{1,0:T(8,128)(2,1)S(1)} %pad_maximum_fusion.4), channel_id=1, source_target_pairs={{0,14},{1,15},{2,0},{3,1},{4,2},{5,3},{6,4},{7,5},{8,6},{9,7},{10,... | collective-permute-start | bytes 884744 | tf_op jit(solution)/shard_map/ppermute | solution.py:11
  67.6 5.7 %collective-permute-done.19 = bf16[128,1152]{1,0:T(8,128)(2,1)S(1)} collective-permute-done((bf16[128,1152]{1,0:T(8,128)(2,1)S(1)}, bf16[128,1152]{1,0:T(8,128)(2,1)S(1)}, u32[]{:S(2)}, u32[]{:S(2)}) %collective-permute-start.19) | collective-permute-done | bytes 294944 | tf_op jit(solution)/shard_map/ppermute | solution.py:11
  73.3 0.1 add_convert_fusion.3
  73.4 0.1 collective-permute-start.20
  73.6 9.2 %collective-permute-done.20 = bf16[128,1152]{1,0:T(8,128)(2,1)S(1)} collective-permute-done((bf16[128,1152]{1,0:T(8,128)(2,1)S(1)}, bf16[128,1152]{1,0:T(8,128)(2,1)S(1)}, u32[]{:S(2)}, u32[]{:S(2)}) %collective-permute-start.20) | collective-permute-done | bytes 294944 | tf_op jit(solution)/shard_map/ppermute | solution.py:11
  82.8 0.1 add_convert_fusion.2
  83.0 0.1 collective-permute-start.24
  83.2 1.5 %collective-permute-start.21 = (bf16[128,1152]{1,0:T(8,128)(2,1)S(1)}, bf16[128,1152]{1,0:T(8,128)(2,1)S(1)}, u32[]{:S(2)}, u32[]{:S(2)}) collective-permute-start(bf16[128,1152]{1,0:T(8,128)(2,1)S(1)} %get-tuple-element.6), channel_id=1, source_target_pairs={{0,2},{1,3},{2,4},{3,5},{4,6},{5,7},{6,8},{7,9},{8,10},{9,11},{10,... | collective-permute-start | bytes 884744 | tf_op jit(solution)/shard_map/ppermute | solution.py:11
  84.7 4.2 %collective-permute-done.24 = bf16[128,1152]{1,0:T(8,128)(2,1)S(1)} collective-permute-done((bf16[128,1152]{1,0:T(8,128)(2,1)S(1)}, bf16[128,1152]{1,0:T(8,128)(2,1)S(1)}, u32[]{:S(2)}, u32[]{:S(2)}) %collective-permute-start.24) | collective-permute-done | bytes 294944 | tf_op jit(solution)/shard_map/ppermute | solution.py:11
  89.0 1.0 collective-permute-start.25
  90.1 1.9 %collective-permute-done.21 = bf16[128,1152]{1,0:T(8,128)(2,1)S(1)} collective-permute-done((bf16[128,1152]{1,0:T(8,128)(2,1)S(1)}, bf16[128,1152]{1,0:T(8,128)(2,1)S(1)}, u32[]{:S(2)}, u32[]{:S(2)}) %collective-permute-start.21) | collective-permute-done | bytes 294944 | tf_op jit(solution)/shard_map/ppermute | solution.py:11
  91.9 2.7 %collective-permute-done.25 = bf16[128,1152]{1,0:T(8,128)(2,1)S(1)} collective-permute-done((bf16[128,1152]{1,0:T(8,128)(2,1)S(1)}, bf16[128,1152]{1,0:T(8,128)(2,1)S(1)}, u32[]{:S(2)}, u32[]{:S(2)}) %collective-permute-start.25) | collective-permute-done | bytes 294944 | tf_op jit(solution)/shard_map/ppermute | solution.py:11
  94.7 0.1 convert_add_fusion
  94.8 13.1 %collective-permute-start.26 = (bf16[64,1152]{1,0:T(8,128)(2,1)S(1)}, bf16[64,1152]{1,0:T(8,128)(2,1)S(1)}, u32[]{:S(2)}, u32[]{:S(2)}) collective-permute-start(bf16[64,1152]{1,0:T(8,128)(2,1)S(1)} %get-tuple-element.25), channel_id=1, source_target_pairs={{0,128},{128,0},{1,129},{129,1},{2,130},{130,2},{3,131},{131,3},{4... | collective-permute-start | bytes 442376 | tf_op jit(solution)/shard_map/ppermute | solution.py:102
  108.0 1.5 %collective-permute-start.27 = (bf16[64,1152]{1,0:T(8,128)(2,1)S(1)}, bf16[64,1152]{1,0:T(8,128)(2,1)S(1)}, u32[]{:S(2)}, u32[]{:S(2)}) collective-permute-start(bf16[64,1152]{1,0:T(8,128)(2,1)S(1)} %get-tuple-element.26), channel_id=1, source_target_pairs={{0,129},{1,128},{2,131},{3,130},{4,133},{5,132},{6,135},{7,134},{8... | collective-permute-start | bytes 442376 | tf_op jit(solution)/shard_map/ppermute | solution.py:106
  109.5 7.4 %fusion = bf16[1,1152,2304]{2,1,0:T(8,128)(2,1)} fusion(bf16[1024,1152]{1,0:T(8,128)(2,1)S(1)} %dynamic-slice_dynamic-update-slice_fusion, bf16[1024,2304]{1,0:T(8,128)(2,1)S(1)} %constant_dynamic-update-slice_fusion.20), kind=kOutput, calls=%fused_computation.1 | convolution fusion | flops 5438472192 | bytes 12386304 | tf_op jit(solution)/shard_map/dot_general | solution.py:116
  116.9 0.7 fusion.80
  (79 shorter events, 1.5 us)
Async XLA Ops:
  0.6 9.0 %copy-start = (bf16[1,64,1152]{2,1,0:T(8,128)(2,1)S(1)}, bf16[1,64,1152]{2,1,0:T(8,128)(2,1)}, u32[]{:S(2)}) copy-start(bf16[1,64,1152]{2,1,0:T(8,128)(2,1)} %param.4) | copy-start | bytes 442372
  0.6 9.0 %collective-permute-start = (bf16[64,1152]{1,0:T(8,128)(2,1)}, bf16[64,1152]{1,0:T(8,128)(2,1)S(1)}, u32[]{:S(2)}, u32[]{:S(2)}) collective-permute-start(bf16[64,1152]{1,0:T(8,128)(2,1)} %bitcast.65), channel_id=1, source_target_pairs={{0,1},{1,0},{2,3},{3,2},{4,5},{5,4},{6,7},{7,6},{8,9},{9,8},{10,11... | collective-permute-start | bytes 442376 | tf_op jit(solution)/shard_map/ppermute | solution.py:16
  6.7 17.4 %collective-permute-start.9 = (bf16[128,2304]{1,0:T(8,128)(2,1)S(1)}, bf16[128,2304]{1,0:T(8,128)(2,1)S(1)}, u32[]{:S(2)}, u32[]{:S(2)}) collective-permute-start(bf16[128,2304]{1,0:T(8,128)(2,1)S(1)} %get-tuple-element.3), channel_id=1, source_target_pairs={{0,16},{16,0},{32,48},{48,32},{64,80},{80,64},{96,112},{112,96},{1... | collective-permute-start | bytes 1769480 | tf_op jit(solution)/shard_map/ppermute | solution.py:16
  7.1 16.4 %collective-permute-start.10 = (bf16[128,2304]{1,0:T(8,128)(2,1)S(1)}, bf16[128,2304]{1,0:T(8,128)(2,1)S(1)}, u32[]{:S(2)}, u32[]{:S(2)}) collective-permute-start(bf16[128,2304]{1,0:T(8,128)(2,1)S(1)} %get-tuple-element.3), channel_id=1, source_target_pairs={{0,96},{16,112},{32,0},{48,16},{64,32},{80,48},{96,64},{112,80},{1... | collective-permute-start | bytes 1769480 | tf_op jit(solution)/shard_map/ppermute | solution.py:11
  9.6 14.5 %collective-permute-start.11 = (bf16[128,2304]{1,0:T(8,128)(2,1)S(1)}, bf16[128,2304]{1,0:T(8,128)(2,1)S(1)}, u32[]{:S(2)}, u32[]{:S(2)}) collective-permute-start(bf16[128,2304]{1,0:T(8,128)(2,1)S(1)} %get-tuple-element.3), channel_id=1, source_target_pairs={{0,32},{16,48},{32,64},{48,80},{64,96},{80,112},{96,0},{112,16},{1... | collective-permute-start | bytes 1769480 | tf_op jit(solution)/shard_map/ppermute | solution.py:11
  9.7 10.4 %collective-permute-start.1 = (bf16[128,1152]{1,0:T(8,128)(2,1)S(1)}, bf16[128,1152]{1,0:T(8,128)(2,1)S(1)}, u32[]{:S(2)}, u32[]{:S(2)}) collective-permute-start(bf16[128,1152]{1,0:T(8,128)(2,1)S(1)} %get-tuple-element.5), channel_id=1, source_target_pairs={{0,14},{1,15},{2,0},{3,1},{4,2},{5,3},{6,4},{7,5},{8,6},{9,7},{10,... | collective-permute-start | bytes 884744 | tf_op jit(solution)/shard_map/ppermute | solution.py:11
  15.3 8.2 %collective-permute-start.4 = (bf16[128,1152]{1,0:T(8,128)(2,1)S(1)}, bf16[128,1152]{1,0:T(8,128)(2,1)S(1)}, u32[]{:S(2)}, u32[]{:S(2)}) collective-permute-start(bf16[128,1152]{1,0:T(8,128)(2,1)S(1)} %get-tuple-element.5), channel_id=1, source_target_pairs={{0,2},{1,3},{2,4},{3,5},{4,6},{5,7},{6,8},{7,9},{8,10},{9,11},{10,... | collective-permute-start | bytes 884744 | tf_op jit(solution)/shard_map/ppermute | solution.py:11
  15.3 12.0 %slice-start.2 = ((s8[4718592]{0:T(1024)(128)(4,1)}), s8[4194304]{0:T(1024)(128)(4,1)S(1)}, s32[]{:S(2)}) async-start(s8[4718592]{0:T(1024)(128)(4,1)} %bitcast.67), calls=%async_computation.2 | async-start | bytes 8388608
  15.4 12.1 %slice-start = ((s8[5308416]{0:T(1024)(128)(4,1)}), s8[4194304]{0:T(1024)(128)(4,1)S(1)}, s32[]{:S(2)}) async-start(s8[5308416]{0:T(1024)(128)(4,1)} %bitcast.63), calls=%async_computation | async-start | bytes 8388608
  15.5 11.9 %slice-start.3 = ((s8[4718592]{0:T(1024)(128)(4,1)}), s8[524288]{0:T(1024)(128)(4,1)S(1)}, s32[]{:S(2)}) async-start(s8[4718592]{0:T(1024)(128)(4,1)} %bitcast.67), calls=%async_computation.3 | async-start | bytes 1048576
  15.5 11.9 %slice-start.1 = ((s8[5308416]{0:T(1024)(128)(4,1)}), s8[1114112]{0:T(1024)(128)(4,1)S(1)}, s32[]{:S(2)}) async-start(s8[5308416]{0:T(1024)(128)(4,1)} %bitcast.63), calls=%async_computation.1 | async-start | bytes 2228224
  20.1 12.8 %collective-permute-start.2 = (bf16[128,1152]{1,0:T(8,128)(2,1)S(1)}, bf16[128,1152]{1,0:T(8,128)(2,1)S(1)}, u32[]{:S(2)}, u32[]{:S(2)}) collective-permute-start(bf16[128,1152]{1,0:T(8,128)(2,1)S(1)} %collective-permute-done.1), channel_id=1, source_target_pairs={{0,14},{1,15},{2,0},{3,1},{4,2},{5,3},{6,4},{7,5},{8,6},{9,7},{10,... | collective-permute-start | bytes 884744 | tf_op jit(solution)/shard_map/ppermute | solution.py:11
  23.5 14.6 %collective-permute-start.5 = (bf16[128,1152]{1,0:T(8,128)(2,1)S(1)}, bf16[128,1152]{1,0:T(8,128)(2,1)S(1)}, u32[]{:S(2)}, u32[]{:S(2)}) collective-permute-start(bf16[128,1152]{1,0:T(8,128)(2,1)S(1)} %collective-permute-done.4), channel_id=1, source_target_pairs={{0,2},{1,3},{2,4},{3,5},{4,6},{5,7},{6,8},{7,9},{8,10},{9,11},{10,... | collective-permute-start | bytes 884744 | tf_op jit(solution)/shard_map/ppermute | solution.py:11
  24.3 23.5 %collective-permute-start.12 = (bf16[128,2304]{1,0:T(8,128)(2,1)S(1)}, bf16[128,2304]{1,0:T(8,128)(2,1)S(1)}, u32[]{:S(2)}, u32[]{:S(2)}) collective-permute-start(bf16[128,2304]{1,0:T(8,128)(2,1)S(1)} %get-tuple-element.28), channel_id=1, source_target_pairs={{0,96},{16,112},{32,0},{48,16},{64,32},{80,48},{96,64},{112,80},{1... | collective-permute-start | bytes 1769480 | tf_op jit(solution)/shard_map/ppermute | solution.py:11
  26.3 21.6 %collective-permute-start.13 = (bf16[128,2304]{1,0:T(8,128)(2,1)S(1)}, bf16[128,2304]{1,0:T(8,128)(2,1)S(1)}, u32[]{:S(2)}, u32[]{:S(2)}) collective-permute-start(bf16[128,2304]{1,0:T(8,128)(2,1)S(1)} %get-tuple-element.29), channel_id=1, source_target_pairs={{0,16},{16,0},{32,48},{48,32},{64,80},{80,64},{96,112},{112,96},{1... | collective-permute-start | bytes 1769480 | tf_op jit(solution)/shard_map/ppermute | solution.py:16
  27.4 20.6 %collective-permute-start.14 = (bf16[128,2304]{1,0:T(8,128)(2,1)S(1)}, bf16[128,2304]{1,0:T(8,128)(2,1)S(1)}, u32[]{:S(2)}, u32[]{:S(2)}) collective-permute-start(bf16[128,2304]{1,0:T(8,128)(2,1)S(1)} %get-tuple-element.27), channel_id=1, source_target_pairs={{0,32},{16,48},{32,64},{48,80},{64,96},{80,112},{96,0},{112,16},{1... | collective-permute-start | bytes 1769480 | tf_op jit(solution)/shard_map/ppermute | solution.py:11
  32.9 12.1 %collective-permute-start.3 = (bf16[128,1152]{1,0:T(8,128)(2,1)S(1)}, bf16[128,1152]{1,0:T(8,128)(2,1)S(1)}, u32[]{:S(2)}, u32[]{:S(2)}) collective-permute-start(bf16[128,1152]{1,0:T(8,128)(2,1)S(1)} %collective-permute-done.2), channel_id=1, source_target_pairs={{0,14},{1,15},{2,0},{3,1},{4,2},{5,3},{6,4},{7,5},{8,6},{9,7},{10,... | collective-permute-start | bytes 884744 | tf_op jit(solution)/shard_map/ppermute | solution.py:11
  38.1 6.8 %collective-permute-start.6 = (bf16[128,1152]{1,0:T(8,128)(2,1)S(1)}, bf16[128,1152]{1,0:T(8,128)(2,1)S(1)}, u32[]{:S(2)}, u32[]{:S(2)}) collective-permute-start(bf16[128,1152]{1,0:T(8,128)(2,1)S(1)} %collective-permute-done.5), channel_id=1, source_target_pairs={{0,2},{1,3},{2,4},{3,5},{4,6},{5,7},{6,8},{7,9},{8,10},{9,11},{10,... | collective-permute-start | bytes 884744 | tf_op jit(solution)/shard_map/ppermute | solution.py:11
  44.9 12.1 %collective-permute-start.7 = (bf16[64,1152]{1,0:T(8,128)(2,1)S(1)}, bf16[64,1152]{1,0:T(8,128)(2,1)S(1)}, u32[]{:S(2)}, u32[]{:S(2)}) collective-permute-start(bf16[64,1152]{1,0:T(8,128)(2,1)S(1)} %slice.62), channel_id=1, source_target_pairs={{0,2},{1,3},{2,4},{3,5},{4,6},{5,7},{6,8},{7,9},{8,10},{9,11},{10,... | collective-permute-start | bytes 442376 | tf_op jit(solution)/shard_map/ppermute | solution.py:11
  45.0 12.0 %collective-permute-start.8 = (bf16[64,1152]{1,0:T(8,128)(2,1)S(1)}, bf16[64,1152]{1,0:T(8,128)(2,1)S(1)}, u32[]{:S(2)}, u32[]{:S(2)}) collective-permute-start(bf16[64,1152]{1,0:T(8,128)(2,1)S(1)} %slice.63), channel_id=1, source_target_pairs={{0,14},{1,15},{2,0},{3,1},{4,2},{5,3},{6,4},{7,5},{8,6},{9,7},{10,... | collective-permute-start | bytes 442376 | tf_op jit(solution)/shard_map/ppermute | solution.py:11
  48.1 9.3 %collective-permute-start.15 = (bf16[128,768]{1,0:T(8,128)(2,1)S(1)}, bf16[128,768]{1,0:T(8,128)(2,1)S(1)}, u32[]{:S(2)}, u32[]{:S(2)}) collective-permute-start(bf16[128,768]{1,0:T(8,128)(2,1)S(1)} %pad_maximum_fusion.7), channel_id=1, source_target_pairs={{0,32},{16,48},{32,64},{48,80},{64,96},{80,112},{96,0},{112,16},{1... | collective-permute-start | bytes 589832 | tf_op jit(solution)/shard_map/ppermute | solution.py:11
  48.2 9.2 %collective-permute-start.17 = (bf16[128,768]{1,0:T(8,128)(2,1)S(1)}, bf16[128,768]{1,0:T(8,128)(2,1)S(1)}, u32[]{:S(2)}, u32[]{:S(2)}) collective-permute-start(bf16[128,768]{1,0:T(8,128)(2,1)S(1)} %pad_maximum_fusion.5), channel_id=1, source_target_pairs={{0,16},{16,0},{32,48},{48,32},{64,80},{80,64},{96,112},{112,96},{1... | collective-permute-start | bytes 589832 | tf_op jit(solution)/shard_map/ppermute | solution.py:16
  48.7 8.7 %collective-permute-start.16 = (bf16[128,768]{1,0:T(8,128)(2,1)S(1)}, bf16[128,768]{1,0:T(8,128)(2,1)S(1)}, u32[]{:S(2)}, u32[]{:S(2)}) collective-permute-start(bf16[128,768]{1,0:T(8,128)(2,1)S(1)} %pad_maximum_fusion.6), channel_id=1, source_target_pairs={{0,96},{16,112},{32,0},{48,16},{64,32},{80,48},{96,64},{112,80},{1... | collective-permute-start | bytes 589832 | tf_op jit(solution)/shard_map/ppermute | solution.py:11
  59.3 5.3 %collective-permute-start.18 = (bf16[64,1152]{1,0:T(8,128)(2,1)S(1)}, bf16[64,1152]{1,0:T(8,128)(2,1)S(1)}, u32[]{:S(2)}, u32[]{:S(2)}) collective-permute-start(bf16[64,1152]{1,0:T(8,128)(2,1)S(1)} %get-tuple-element.10), channel_id=1, source_target_pairs={{0,2},{1,3},{2,4},{3,5},{4,6},{5,7},{6,8},{7,9},{8,10},{9,11},{10,... | collective-permute-start | bytes 442376 | tf_op jit(solution)/shard_map/ppermute | solution.py:11
  59.4 5.2 %collective-permute-start.22 = (bf16[64,1152]{1,0:T(8,128)(2,1)S(1)}, bf16[64,1152]{1,0:T(8,128)(2,1)S(1)}, u32[]{:S(2)}, u32[]{:S(2)}) collective-permute-start(bf16[64,1152]{1,0:T(8,128)(2,1)S(1)} %get-tuple-element.11), channel_id=1, source_target_pairs={{0,14},{1,15},{2,0},{3,1},{4,2},{5,3},{6,4},{7,5},{8,6},{9,7},{10,... | collective-permute-start | bytes 442376 | tf_op jit(solution)/shard_map/ppermute | solution.py:11
  64.7 8.6 %collective-permute-start.19 = (bf16[128,1152]{1,0:T(8,128)(2,1)S(1)}, bf16[128,1152]{1,0:T(8,128)(2,1)S(1)}, u32[]{:S(2)}, u32[]{:S(2)}) collective-permute-start(bf16[128,1152]{1,0:T(8,128)(2,1)S(1)} %pad_maximum_fusion.3), channel_id=1, source_target_pairs={{0,2},{1,3},{2,4},{3,5},{4,6},{5,7},{6,8},{7,9},{8,10},{9,11},{10,... | collective-permute-start | bytes 884744 | tf_op jit(solution)/shard_map/ppermute | solution.py:11
  64.8 8.7 %collective-permute-start.23 = (bf16[128,1152]{1,0:T(8,128)(2,1)S(1)}, bf16[128,1152]{1,0:T(8,128)(2,1)S(1)}, u32[]{:S(2)}, u32[]{:S(2)}) collective-permute-start(bf16[128,1152]{1,0:T(8,128)(2,1)S(1)} %pad_maximum_fusion.4), channel_id=1, source_target_pairs={{0,14},{1,15},{2,0},{3,1},{4,2},{5,3},{6,4},{7,5},{8,6},{9,7},{10,... | collective-permute-start | bytes 884744 | tf_op jit(solution)/shard_map/ppermute | solution.py:11
  73.4 9.4 %collective-permute-start.20 = (bf16[128,1152]{1,0:T(8,128)(2,1)S(1)}, bf16[128,1152]{1,0:T(8,128)(2,1)S(1)}, u32[]{:S(2)}, u32[]{:S(2)}) collective-permute-start(bf16[128,1152]{1,0:T(8,128)(2,1)S(1)} %add_convert_fusion.3), channel_id=1, source_target_pairs={{0,2},{1,3},{2,4},{3,5},{4,6},{5,7},{6,8},{7,9},{8,10},{9,11},{10,... | collective-permute-start | bytes 884744 | tf_op jit(solution)/shard_map/ppermute | solution.py:11
  83.0 5.9 %collective-permute-start.24 = (bf16[128,1152]{1,0:T(8,128)(2,1)S(1)}, bf16[128,1152]{1,0:T(8,128)(2,1)S(1)}, u32[]{:S(2)}, u32[]{:S(2)}) collective-permute-start(bf16[128,1152]{1,0:T(8,128)(2,1)S(1)} %get-tuple-element.7), channel_id=1, source_target_pairs={{0,14},{1,15},{2,0},{3,1},{4,2},{5,3},{6,4},{7,5},{8,6},{9,7},{10,... | collective-permute-start | bytes 884744 | tf_op jit(solution)/shard_map/ppermute | solution.py:11
  83.2 8.8 %collective-permute-start.21 = (bf16[128,1152]{1,0:T(8,128)(2,1)S(1)}, bf16[128,1152]{1,0:T(8,128)(2,1)S(1)}, u32[]{:S(2)}, u32[]{:S(2)}) collective-permute-start(bf16[128,1152]{1,0:T(8,128)(2,1)S(1)} %get-tuple-element.6), channel_id=1, source_target_pairs={{0,2},{1,3},{2,4},{3,5},{4,6},{5,7},{6,8},{7,9},{8,10},{9,11},{10,... | collective-permute-start | bytes 884744 | tf_op jit(solution)/shard_map/ppermute | solution.py:11
  89.0 5.7 %collective-permute-start.25 = (bf16[128,1152]{1,0:T(8,128)(2,1)S(1)}, bf16[128,1152]{1,0:T(8,128)(2,1)S(1)}, u32[]{:S(2)}, u32[]{:S(2)}) collective-permute-start(bf16[128,1152]{1,0:T(8,128)(2,1)S(1)} %add_convert_fusion), channel_id=1, source_target_pairs={{0,14},{1,15},{2,0},{3,1},{4,2},{5,3},{6,4},{7,5},{8,6},{9,7},{10,... | collective-permute-start | bytes 884744 | tf_op jit(solution)/shard_map/ppermute | solution.py:11
  94.8 22.1 %collective-permute-start.26 = (bf16[64,1152]{1,0:T(8,128)(2,1)S(1)}, bf16[64,1152]{1,0:T(8,128)(2,1)S(1)}, u32[]{:S(2)}, u32[]{:S(2)}) collective-permute-start(bf16[64,1152]{1,0:T(8,128)(2,1)S(1)} %get-tuple-element.25), channel_id=1, source_target_pairs={{0,128},{128,0},{1,129},{129,1},{2,130},{130,2},{3,131},{131,3},{4... | collective-permute-start | bytes 442376 | tf_op jit(solution)/shard_map/ppermute | solution.py:102
  108.0 9.0 %collective-permute-start.27 = (bf16[64,1152]{1,0:T(8,128)(2,1)S(1)}, bf16[64,1152]{1,0:T(8,128)(2,1)S(1)}, u32[]{:S(2)}, u32[]{:S(2)}) collective-permute-start(bf16[64,1152]{1,0:T(8,128)(2,1)S(1)} %get-tuple-element.26), channel_id=1, source_target_pairs={{0,129},{1,128},{2,131},{3,130},{4,133},{5,132},{6,135},{7,134},{8... | collective-permute-start | bytes 442376 | tf_op jit(solution)/shard_map/ppermute | solution.py:106

commit v2 on v0

v2 whole, which is shorter than its diff:
```python
import jax
import jax.numpy as jnp
from jax import lax
from jax.experimental import pallas as pl
from jax.experimental.pallas import tpu as pltpu
from jax.sharding import PartitionSpec as P

F32, BF16 = jnp.float32, jnp.bfloat16
Z, DP, T, S = 8, 8, 16, 2
together = lax.optimization_barrier
OVER_LAST = (((1,), (1,)), ((), ()))


def shift(block, axis, distance):
    n = lax.axis_size(axis)
    return lax.ppermute(block, axis, [(i, (i + distance) % n) for i in range(n)])


def swap(block, axis):
    n = lax.axis_size(axis)
    return lax.ppermute(block, axis, [(i, i ^ 1) for i in range(n)])


def along_z(blocks, distance):
    route = []
    for s in range(S):
        for t in range(T):
            to = (t + 2 * (distance if s == 0 else -distance)) % T
            route.append((s * T + t, s * T + to))
    return lax.ppermute(blocks, ("section", "tensor"), route)


def deliver(block, dz, flip):
    route = []
    for s in range(S):
        for t in range(T):
            to = ((t // 2 + dz) % Z) * 2 + (t % 2 ^ flip)
            route.append((s * T + t, (1 - s) * T + to))
    return lax.ppermute(block, ("section", "tensor"), route)


def times_kernel(block_ref, weight_ref, out_ref):
    wide = weight_ref.shape[0]
    for start in range(0, wide, 256):
        stop = min(start + 256, wide)
        out_ref[:, start:stop] = lax.dot_general(
            block_ref[...],
            weight_ref[start:stop, :],
            (((1,), (1,)), ((), ())),
            preferred_element_type=F32,
        ).astype(out_ref.dtype)


def times(block, weight):
    rows, depth = block.shape
    wide = weight.shape[0]
    return pl.pallas_call(
        times_kernel,
        in_specs=[pl.BlockSpec(memory_space=pltpu.VMEM)] * 2,
        out_specs=pl.BlockSpec(memory_space=pltpu.VMEM),
        out_shape=jax.ShapeDtypeStruct((rows, wide), BF16),
        cost_estimate=pl.CostEstimate(
            flops=2 * rows * depth * wide,
            bytes_accessed=2 * (rows * depth + wide * depth + rows * wide),
            transcendentals=0,
        ),
        compiler_params=pltpu.CompilerParams(vmem_limit_bytes=8 * 2**20),
        name="times",
    )(block, weight)


def place(dx, dy):
    dp = lax.axis_index("dp")
    return ((dp // 2 + dx) % 4) * 2 + (dp % 2 + dy) % 2


FIRST = ((0, 0), (0, 1), (1, 0), (3, 0))
SECOND = ((1, 1), (2, 0), (3, 1))
FAR = ((2, 1),)


def far_kernel(first_ref, second_ref, left_ref, right_ref, weight_ref, out_ref):
    tensor = lax.axis_index("tensor")
    z, y_hi = tensor // 2, tensor % 2
    rows, middle = left_ref.shape
    half = rows // 2

    def fill(which, source, index, columns=slice(None)):
        block = ((place(*which) - z + Z) % Z) * rows
        for high in range(2):
            away = y_hi if high == 0 else 1 - y_hi
            where = pl.multiple_of(block + away * half, half)
            begin = index * rows + high * half
            out_ref[pl.ds(where, half), columns] = source[begin : begin + half, :]

    for i, which in enumerate(FIRST):
        fill(which, first_ref, i)
    for i, which in enumerate(SECOND):
        fill(which, second_ref, i)
    wide = weight_ref.shape[0]
    for start in range(0, wide, 256):
        some = slice(start, min(start + 256, wide))
        total = lax.dot_general(
            left_ref[...], weight_ref[some, :middle], OVER_LAST, preferred_element_type=F32
        )
        total += lax.dot_general(
            right_ref[...], weight_ref[some, middle:], OVER_LAST, preferred_element_type=F32
        )
        fill(FAR[0], total.astype(out_ref.dtype), 0, some)


def all_terms(first, second, left, right, weight):
    rows, middle = left.shape
    wide = weight.shape[0]
    return pl.pallas_call(
        far_kernel,
        in_specs=[pl.BlockSpec(memory_space=pltpu.VMEM)] * 5,
        out_specs=pl.BlockSpec(memory_space=pltpu.VMEM),
        out_shape=jax.ShapeDtypeStruct((DP * rows, wide), BF16),
        cost_estimate=pl.CostEstimate(
            flops=4 * rows * middle * wide,
            bytes_accessed=2 * (2 * rows * middle + 2 * wide * middle + 2 * DP * rows * wide),
            transcendentals=0,
        ),
        compiler_params=pltpu.CompilerParams(vmem_limit_bytes=8 * 2**20),
        name="all_terms",
    )(first, second, left, right, weight)


def weight_kernel(*refs):
    blocks, pieces = refs[:9], refs[9:15]
    out_ref, token_ref, grads, inputs = refs[15:]
    own, beside, right, left, from_left, from_right, from_beside, far_left, far_right = blocks
    half = own.shape[0] // 2
    middle = far_left.shape[1]
    step = out_ref.shape[0]

    @pl.when(pl.program_id(0) == 0)
    def _():
        tensor, section = lax.axis_index("tensor"), lax.axis_index("section")
        z, y_hi = tensor // 2, tensor % 2
        token_ref[...] = jnp.zeros_like(token_ref)

        def fill(spot, high, source, part, columns=slice(None)):
            apart = z - place(*(FIRST + SECOND + FAR)[spot])
            order = (apart * (1 - 2 * section) + Z) % Z
            away = y_hi if high == 0 else 1 - y_hi
            where = pl.multiple_of((order + away * Z) * half, half)
            grads[pl.ds(where, half), columns] = source[part * half : (part + 1) * half, :]

        for spot, block in enumerate((own, beside, right, left)):
            fill(spot, 0, block, 0)
            fill(spot, 1, block, 1)
        fill(4, 0, from_right, 1)
        fill(4, 1, from_beside, 1)
        fill(5, 0, from_left, 0)
        fill(5, 1, from_right, 0)
        fill(6, 0, from_left, 1)
        fill(6, 1, from_beside, 0)
        for block, columns in ((far_left, slice(0, middle)), (far_right, slice(middle, None))):
            fill(7, 0, block, 0, columns)
            fill(7, 1, block, 1, columns)
        start = 0
        for block in pieces:
            inputs[start : start + block.shape[0], :] = block[...]
            start += block.shape[0]

    columns = pl.ds(pl.multiple_of(pl.program_id(0) * step, step), step)
    part = inputs[:, columns].T
    wide = grads.shape[1]
    for start in range(0, wide, wide // 3):
        some = slice(start, start + wide // 3)
        out_ref[:, some] = jnp.dot(
            part, grads[:, some], preferred_element_type=F32
        ).astype(out_ref.dtype)


def weight_times(blocks, inputs):
    rows, depth = 8 * blocks[0].shape[0], blocks[0].shape[1]
    wide = inputs[0].shape[1]
    step = wide // 3
    return pl.pallas_call(
        weight_kernel,
        grid=(wide // step,),
        in_specs=[pl.BlockSpec(memory_space=pltpu.VMEM)] * (len(blocks) + len(inputs)),
        out_specs=(
            pl.BlockSpec((step, depth), lambda i: (i, 0)),
            pl.BlockSpec((8, 128), lambda i: (0, 0)),
        ),
        out_shape=(
            jax.ShapeDtypeStruct((wide, depth), BF16),
            jax.ShapeDtypeStruct((8, 128), F32),
        ),
        scratch_shapes=[
            pltpu.VMEM((rows, depth), BF16),
            pltpu.VMEM((rows, wide), BF16),
        ],
        cost_estimate=pl.CostEstimate(
            flops=2 * rows * depth * wide,
            bytes_accessed=2 * (rows * depth + wide * depth + rows * wide),
            transcendentals=0,
        ),
        compiler_params=pltpu.CompilerParams(vmem_limit_bytes=16 * 2**20),
        name="weight_times",
    )(*blocks, *inputs)


def on_device(layer_inputs, projection, pre_act, act_grad):
    weight = projection[0]
    rows = pre_act.shape[1]
    half = rows // 2
    middle = pre_act.shape[2] // 2
    wide = weight.shape[0]

    beneath = along_z(layer_inputs[0], 1)

    own = (
        2.0 * jnp.maximum(pre_act[0].astype(F32), 0.0) * act_grad[0].astype(F32)
    ).astype(BF16)

    left = shift(own, "dp", 2)
    right = shift(own, "dp", -2)
    beside = swap(own, "dp")
    held = jnp.concatenate([layer_inputs[0], beneath])
    near = along_z(held, 2)
    last = along_z(held, -2)
    left, right, beside = together((left, right, beside))

    from_left = shift(jnp.concatenate([left[:half], beside[:half]]), "dp", 2)
    from_right = shift(jnp.concatenate([right[half:], beside[:half]]), "dp", -2)
    from_beside = swap(jnp.concatenate([left[half:], right[half:]]), "dp")

    first_part = times(jnp.concatenate([own, beside, right, left]), weight)
    last, first_part = together((last, first_part))
    beyond = along_z(last, -2)

    from_left, from_right, from_beside, near, beyond = together(
        (from_left, from_right, from_beside, near, beyond)
    )
    across = jnp.concatenate([from_left[:half], from_right[:half]])
    left_beside = jnp.concatenate([from_left[half:], from_beside[:half]])
    right_beside = jnp.concatenate([from_right[half:], from_beside[half:]])
    far_left = shift(left_beside[:, :middle], "dp", 2)
    far_right = shift(right_beside[:, middle:], "dp", -2)

    second_part = times(jnp.concatenate([right_beside, across, left_beside]), weight)
    held, second_part = together((held, second_part))
    held_away = swap(jnp.concatenate([held, near]), "tensor")

    terms = all_terms(first_part, second_part, far_left, far_right, weight)
    beyond, terms = together((beyond, terms))
    beyond_away = swap(jnp.concatenate([beyond, last]), "tensor")

    def term(step):
        begin = step % Z * rows
        return terms[begin : begin + rows].astype(F32)

    def along(total, direction):
        return shift(total.astype(BF16), "tensor", 2 * direction)

    def both(same, away):
        return jnp.concatenate([same, away])

    up, down = along(term(4)[:half], 1), along(term(4)[half:], -1)
    up, down = together((up, down))

    up, down = up.astype(F32), down.astype(F32)
    up = both(term(3)[:half] + up, term(3)[half:])
    down = both(term(-3)[:half], term(-3)[half:] + down)
    up, down = along(up, 1), along(down, -1)
    held_away, own_term = together((held_away, term(0).astype(BF16)))
    pieces = [deliver(own_term[:half], 0, 0), deliver(own_term[half:], 0, 1)]
    up, down, beyond_away = together((up, down, beyond_away))

    up = along(term(2) + up.astype(F32), 1)
    down = along(term(-2) + down.astype(F32), -1)
    weight_grad, zeros = weight_times(
        (own, beside, right, left, from_left, from_right, from_beside, far_left, far_right),
        (held, near, beyond, last, held_away, beyond_away),
    )
    up, down, zeros, *pieces = together((up, down, zeros, *pieces))
    up, down = up.astype(F32) + zeros[:1, :1], down.astype(F32)

    for total, dz in ((term(1) + up, 1), (term(-1) + down, -1)):
        total = total.astype(BF16)
        pieces += [deliver(total[:half], dz, 0), deliver(total[half:], dz, 1)]
    handed = sum(piece.astype(F32) for piece in pieces).astype(BF16)
    return (weight_grad[None], handed[None])


def solution(mesh):
    return jax.shard_map(
        on_device,
        mesh=mesh,
        in_specs=(
            P("section", "tensor", "dp"),
            P("section", "dp", "tensor"),
            P("section", "dp", "tensor"),
            P("section", "dp", "tensor"),
        ),
        out_specs=(P("section", "dp", "tensor"), P("section", "tensor", "dp")),
        check_vma=False,
    )
```

time: 453 us -> 107 us (0.24)
  waiting for transfers between devices: 399 us -> 24.3 us
  starting transfers between devices: 4.81 us -> 60.8 us
  matrix products: 21.2 us -> 0 us
  Pallas kernels: 0 us -> 15.5 us
  between operations: 13.7 us -> 0.91 us
  local copies, waits for them, and re-layouts: 9.2 us -> 1.37 us
    reduce_scatter x1 -> x0, waiting for transfers between devices: 208 us -> none  [on_device(): lax.psum_scatter(lax.dot_general(all_grads, weight, (((1,), (1,)), ((), (...]
    all_gather x2 -> x0, waiting for transfers between devices: 190 us -> none  [the longest x1 107 us: on_device(): all_grads = lax.all_gather(pre_grad, 'dp', axis=0, tiled=True)]
    ppermute x1 -> x26, starting transfers between devices: 4.69 us -> 60.8 us  [the longest x6 25.6 us: deliver(): return lax.ppermute(block, ('section', 'tensor'), route)]
    ppermute x1 -> x26, waiting for transfers between devices: 0.01 us -> 24.3 us  [the longest x4 9.84 us: along_z(): return lax.ppermute(blocks, ('section', 'tensor'), route)]
    dot_general x2 -> x0, matrix products: 21.2 us -> none  [the longest x1 10.7 us: on_device(): lax.dot_general(all_grads, weight, (((1,), (1,)), ((), ())), preferred_el...]
    pallas_call x0 -> x4, Pallas kernels: none -> 15.5 us  [the longest x1 7.89 us: weight_times(): pl.pallas_call(weight_kernel, grid=(wide // step,), in_specs=[pl.BlockSpe...]
    unnamed x2 -> x11, local copies, waits for them, and re-layouts: 9.2 us -> 0.57 us
  transfers between devices with their start and end apart: 4 -> 26, of which waited for: 3 -> 9; matrix products, arithmetic and copies ran while one was open for 4% -> 1% of each run, Pallas kernels for 0% -> 15%
where the time goes in v2:
time: 107 us
  starting transfers between devices  60.8 us (57%)
  waiting for transfers between devices  24.3 us (23%)
  Pallas kernels  15.5 us (14%)
  other arithmetic  3.78 us (4%)
  local copies, waits for them, and re-layouts  1.37 us (1%)
    ppermute x6, starting transfers between devices, deliver(): return lax.ppermute(block, ('section', 'tensor'), route)  25.6 us
    ppermute x12, starting transfers between devices, shift(): lax.ppermute(block, axis, [(i, (i + distance) % n) for i in range(n)])  14.6 us
    ppermute x4, starting transfers between devices, along_z(): return lax.ppermute(blocks, ('section', 'tensor'), route)  12.3 us
    ppermute x4, waiting for transfers between devices, along_z(): return lax.ppermute(blocks, ('section', 'tensor'), route)  9.84 us
    ppermute x4, starting transfers between devices, swap(): return lax.ppermute(block, axis, [(i, i ^ 1) for i in range(n)])  8.32 us
    pallas_call x1, Pallas kernels, weight_times(): pl.pallas_call(weight_kernel, grid=(wide // step,), in_specs=[pl.BlockSpe...  7.89 us
    ppermute x6, waiting for transfers between devices, deliver(): return lax.ppermute(block, ('section', 'tensor'), route)  7.48 us
    ppermute x12, waiting for transfers between devices, shift(): lax.ppermute(block, axis, [(i, (i + distance) % n) for i in range(n)])  6.92 us
  transfers between devices with their start and end apart: 26, of which 9 were waited for; matrix products, arithmetic and copies ran while one was open for 1% of the time, Pallas kernels for 15%

profile of v2, /device:TPU:1, one launch (start us, length us, event | category | flops | bytes accessed | tf_op | source)
XLA Modules:
  0.0 106.6 jit_solution(8968117895179287210)
XLA Ops:
  0.6 1.5 %fusion.refs_0_ = bf16[128,2304]{1,0:T(8,128)(2,1)S(1)} fusion(bf16[1,128,2304]{2,1,0:T(8,128)(2,1)} %param.7, bf16[1,128,2304]{2,1,0:T(8,128)(2,1)} %param.6), kind=kLoop, calls=%fused_computation.4 | loop fusion | flops 1769472 | bytes 1769472 | tf_op jit(solution)/shard_map/mul | solution.py:218
  2.1 2.2 %collective-permute-start.2 = (bf16[128,2304]{1,0:T(8,128)(2,1)S(1)}, bf16[128,2304]{1,0:T(8,128)(2,1)S(1)}, u32[]{:S(2)}, u32[]{:S(2)}) collective-permute-start(bf16[128,2304]{1,0:T(8,128)(2,1)S(1)} %fusion.refs_0_), channel_id=1, source_target_pairs={{0,16},{16,0},{32,48},{48,32},{64,80},{80,64},{96,112},{112,96},{1... | collective-permute-start | bytes 1769480 | tf_op jit(solution)/shard_map/ppermute | solution.py:21
  4.3 2.5 %collective-permute-start.1 = (bf16[128,2304]{1,0:T(8,128)(2,1)S(1)}, bf16[128,2304]{1,0:T(8,128)(2,1)S(1)}, u32[]{:S(2)}, u32[]{:S(2)}) collective-permute-start(bf16[128,2304]{1,0:T(8,128)(2,1)S(1)} %fusion.refs_0_), channel_id=1, source_target_pairs={{0,96},{16,112},{32,0},{48,16},{64,32},{80,48},{96,64},{112,80},{1... | collective-permute-start | bytes 1769480 | tf_op jit(solution)/shard_map/ppermute | solution.py:16
  6.8 5.6 %collective-permute-start.6 = (bf16[64,1152]{1,0:T(8,128)(2,1)S(1)}, bf16[64,1152]{1,0:T(8,128)(2,1)S(1)}, u32[]{:S(2)}, u32[]{:S(2)}) collective-permute-start(bf16[64,1152]{1,0:T(8,128)(2,1)S(1)} %bitcast.13), channel_id=1, source_target_pairs={{0,2},{1,3},{2,4},{3,5},{4,6},{5,7},{6,8},{7,9},{8,10},{9,11},{10,... | collective-permute-start | bytes 442376 | tf_op jit(solution)/shard_map/ppermute | solution.py:30
  12.4 2.1 %collective-permute-done.6 = bf16[64,1152]{1,0:T(8,128)(2,1)S(1)} collective-permute-done((bf16[64,1152]{1,0:T(8,128)(2,1)S(1)}, bf16[64,1152]{1,0:T(8,128)(2,1)S(1)}, u32[]{:S(2)}, u32[]{:S(2)}) %collective-permute-start.6) | collective-permute-done | bytes 147488 | tf_op jit(solution)/shard_map/ppermute | solution.py:30
  14.5 0.1 collective-permute-start.8
  14.6 3.6 %collective-permute-start.7 = (bf16[128,1152]{1,0:T(8,128)(2,1)S(1)}, bf16[128,1152]{1,0:T(8,128)(2,1)S(1)}, u32[]{:S(2)}, u32[]{:S(2)}) collective-permute-start(bf16[128,1152]{1,0:T(8,128)(2,1)S(1)} %pad_maximum_fusion.8.refs_9_), channel_id=1, source_target_pairs={{0,4},{1,5},{2,6},{3,7},{4,8},{5,9},{6,10},{7,11},{8,12},{9,13},{1... | collective-permute-start | bytes 884744 | tf_op jit(solution)/shard_map/ppermute | solution.py:30
  18.2 0.3 collective-permute-done.1.refs_2_
  18.5 3.1 %collective-permute-done.refs_3_ = bf16[128,2304]{1,0:T(8,128)(2,1)S(1)} collective-permute-done((bf16[128,2304]{1,0:T(8,128)(2,1)S(1)}, bf16[128,2304]{1,0:T(8,128)(2,1)S(1)}, u32[]{:S(2)}, u32[]{:S(2)}) %collective-permute-start) | collective-permute-done | bytes 589856 | tf_op jit(solution)/shard_map/ppermute | solution.py:16
  21.7 0.0 slice-start.1
  21.7 0.1 pad_maximum_fusion.3
  21.9 0.3 collective-permute-start.5
  22.1 0.3 collective-permute-start.4
  22.4 1.2 %collective-permute-start.3 = (bf16[128,2304]{1,0:T(8,128)(2,1)S(1)}, bf16[128,2304]{1,0:T(8,128)(2,1)S(1)}, u32[]{:S(2)}, u32[]{:S(2)}) collective-permute-start(bf16[128,2304]{1,0:T(8,128)(2,1)S(1)} %get-tuple-element.85), channel_id=1, source_target_pairs={{0,32},{16,48},{32,64},{48,80},{64,96},{80,112},{96,0},{112,16},{1... | collective-permute-start | bytes 1769480 | tf_op jit(solution)/shard_map/ppermute | solution.py:16
  23.6 0.2 pad_maximum_fusion.block_ref
  23.7 0.1 slice-done
  23.8 0.3 slice-done.1
  24.2 3.2 %times.2.first_ref = bf16[512,1152]{1,0:T(8,128)(2,1)S(1)} custom-call(bf16[512,2304]{1,0:T(8,128)(2,1)S(1)} %pad_maximum_fusion.block_ref, bf16[1152,2304]{1,0:T(8,128)(2,1)S(1)} %bitcast.10), custom_call_target="tpu_custom_call" | custom-call | flops 2717908992 | bytes 8847360 | tf_op jit(solution)/shard_map/times/pallas_call | solution.py:57
  27.4 3.1 %collective-permute-start.9 = (bf16[128,1152]{1,0:T(8,128)(2,1)S(1)}, bf16[128,1152]{1,0:T(8,128)(2,1)S(1)}, u32[]{:S(2)}, u32[]{:S(2)}) collective-permute-start(bf16[128,1152]{1,0:T(8,128)(2,1)S(1)} %collective-permute-done.8.refs_12_), channel_id=1, source_target_pairs={{0,12},{1,13},{2,14},{3,15},{4,0},{5,1},{6,2},{7,3},{8,4},{9,5},{1... | collective-permute-start | bytes 884744 | tf_op jit(solution)/shard_map/ppermute | solution.py:30
  30.5 1.7 %collective-permute-done.7.refs_10_ = bf16[128,1152]{1,0:T(8,128)(2,1)S(1)} collective-permute-done((bf16[128,1152]{1,0:T(8,128)(2,1)S(1)}, bf16[128,1152]{1,0:T(8,128)(2,1)S(1)}, u32[]{:S(2)}, u32[]{:S(2)}) %collective-permute-start.7) | collective-permute-done | bytes 294944 | tf_op jit(solution)/shard_map/ppermute | solution.py:30
  32.2 6.0 %collective-permute-done.9.refs_11_ = bf16[128,1152]{1,0:T(8,128)(2,1)S(1)} collective-permute-done((bf16[128,1152]{1,0:T(8,128)(2,1)S(1)}, bf16[128,1152]{1,0:T(8,128)(2,1)S(1)}, u32[]{:S(2)}, u32[]{:S(2)}) %collective-permute-start.9) | collective-permute-done | bytes 294944 | tf_op jit(solution)/shard_map/ppermute | solution.py:30
  38.4 0.1 constant_dynamic-update-slice_fusion
  38.5 1.2 %collective-permute-start.11 = (bf16[128,1152]{1,0:T(8,128)(2,1)S(1)}, bf16[128,1152]{1,0:T(8,128)(2,1)S(1)}, u32[]{:S(2)}, u32[]{:S(2)}) collective-permute-start(bf16[128,1152]{1,0:T(8,128)(2,1)S(1)} %pad_maximum_fusion.6), channel_id=1, source_target_pairs={{0,96},{16,112},{32,0},{48,16},{64,32},{80,48},{96,64},{112,80},{1... | collective-permute-start | bytes 884744 | tf_op jit(solution)/shard_map/ppermute | solution.py:16
  39.7 0.6 collective-permute-start.10
  40.3 2.5 %times.3.second_ref = bf16[384,1152]{1,0:T(8,128)(2,1)S(1)} custom-call(bf16[384,2304]{1,0:T(8,128)(2,1)S(1)} %get-tuple-element.68.block_ref, bf16[1152,2304]{1,0:T(8,128)(2,1)S(1)} %bitcast.11), custom_call_target="tpu_custom_call" | custom-call | flops 2038431744 | bytes 7962624 | tf_op jit(solution)/shard_map/times/pallas_call | solution.py:57
  42.9 2.7 %collective-permute-start.12 = (bf16[256,1152]{1,0:T(8,128)(2,1)S(1)}, bf16[256,1152]{1,0:T(8,128)(2,1)S(1)}, u32[]{:S(2)}, u32[]{:S(2)}) collective-permute-start(bf16[256,1152]{1,0:T(8,128)(2,1)S(1)} %pad_maximum_fusion.4), channel_id=1, source_target_pairs={{0,1},{1,0},{2,3},{3,2},{4,5},{5,4},{6,7},{7,6},{8,9},{9,8},{10,11... | collective-permute-start | bytes 1769480 | tf_op jit(solution)/shard_map/ppermute | solution.py:21
  45.6 1.2 %collective-permute-done.10.left_ref.refs_7_ = bf16[128,1152]{1,0:T(8,128)(2,1)S(1)} collective-permute-done((bf16[128,1152]{1,0:T(8,128)(2,1)S(1)}, bf16[128,1152]{1,0:T(8,128)(2,1)S(1)}, u32[]{:S(2)}, u32[]{:S(2)}) %collective-permute-start.10) | collective-permute-done | bytes 294944 | tf_op jit(solution)/shard_map/ppermute | solution.py:16
  46.8 1.9 %all_terms.1 = bf16[1024,1152]{1,0:T(8,128)(2,1)S(1)} custom-call(bf16[512,1152]{1,0:T(8,128)(2,1)S(1)} %times.2.first_ref, bf16[384,1152]{1,0:T(8,128)(2,1)S(1)} %times.3.second_ref, bf16[128,1152]{1,0:T(8,128)(2,1)S(1)} %collective-permute-done.10.left_ref.refs_7_, bf16[128,1152]{1,0:T(8,128)(2,1)S(1)} %collective-permute-done.11.right_ref.refs_8_, ...), custom_call_target="tpu_custom_call" | custom-call | flops 679477248 | bytes 10616832 | tf_op jit(solution)/shard_map/all_terms/pallas_call | solution.py:115
  48.8 4.5 %collective-permute-start.14 = (bf16[64,1152]{1,0:T(8,128)(2,1)S(1)}, bf16[64,1152]{1,0:T(8,128)(2,1)S(1)}, u32[]{:S(2)}, u32[]{:S(2)}) collective-permute-start(bf16[64,1152]{1,0:T(8,128)(2,1)S(1)} %get-tuple-element.64), channel_id=1, source_target_pairs={{0,14},{1,15},{2,0},{3,1},{4,2},{5,3},{6,4},{7,5},{8,6},{9,7},{10,... | collective-permute-start | bytes 442376 | tf_op jit(solution)/shard_map/ppermute | solution.py:16
  53.3 3.1 %collective-permute-start.17 = (bf16[256,1152]{1,0:T(8,128)(2,1)S(1)}, bf16[256,1152]{1,0:T(8,128)(2,1)S(1)}, u32[]{:S(2)}, u32[]{:S(2)}) collective-permute-start(bf16[256,1152]{1,0:T(8,128)(2,1)S(1)} %pad_maximum_fusion.5), channel_id=1, source_target_pairs={{0,1},{1,0},{2,3},{3,2},{4,5},{5,4},{6,7},{7,6},{8,9},{9,8},{10,11... | collective-permute-start | bytes 1769480 | tf_op jit(solution)/shard_map/ppermute | solution.py:21
  56.5 2.3 %collective-permute-done.13 = bf16[64,1152]{1,0:T(8,128)(2,1)S(1)} collective-permute-done((bf16[64,1152]{1,0:T(8,128)(2,1)S(1)}, bf16[64,1152]{1,0:T(8,128)(2,1)S(1)}, u32[]{:S(2)}, u32[]{:S(2)}) %collective-permute-start.13) | collective-permute-done | bytes 147488 | tf_op jit(solution)/shard_map/ppermute | solution.py:16
  58.7 0.1 add_convert_fusion.5
  58.9 0.1 collective-permute-start.15
  59.0 2.7 %collective-permute-start.16 = (bf16[128,1152]{1,0:T(8,128)(2,1)S(1)}, bf16[128,1152]{1,0:T(8,128)(2,1)S(1)}, u32[]{:S(2)}, u32[]{:S(2)}) collective-permute-start(bf16[128,1152]{1,0:T(8,128)(2,1)S(1)} %pad_maximum_fusion.10), channel_id=1, source_target_pairs={{0,14},{1,15},{2,0},{3,1},{4,2},{5,3},{6,4},{7,5},{8,6},{9,7},{10,... | collective-permute-start | bytes 884744 | tf_op jit(solution)/shard_map/ppermute | solution.py:16
  61.7 12.7 %collective-permute-start.21 = (bf16[64,1152]{1,0:T(8,128)(2,1)S(1)}, bf16[64,1152]{1,0:T(8,128)(2,1)S(1)}, u32[]{:S(2)}, u32[]{:S(2)}) collective-permute-start(bf16[64,1152]{1,0:T(8,128)(2,1)S(1)} %get-tuple-element.81), channel_id=1, source_target_pairs={{0,129},{1,128},{2,131},{3,130},{4,133},{5,132},{6,135},{7,134},{8... | collective-permute-start | bytes 442376 | tf_op jit(solution)/shard_map/ppermute | solution.py:39
  74.4 0.1 add_convert_fusion.2
  74.6 0.1 collective-permute-start.19
  74.7 1.5 %collective-permute-start.18 = (bf16[128,1152]{1,0:T(8,128)(2,1)S(1)}, bf16[128,1152]{1,0:T(8,128)(2,1)S(1)}, u32[]{:S(2)}, u32[]{:S(2)}) collective-permute-start(bf16[128,1152]{1,0:T(8,128)(2,1)S(1)} %get-tuple-element.61), channel_id=1, source_target_pairs={{0,2},{1,3},{2,4},{3,5},{4,6},{5,7},{6,8},{7,9},{8,10},{9,11},{10,... | collective-permute-start | bytes 884744 | tf_op jit(solution)/shard_map/ppermute | solution.py:16
  76.1 7.9 %weight_times.1 = (bf16[1152,2304]{1,0:T(8,128)(2,1)}, f32[8,128]{1,0:T(8,128)S(1)}) custom-call(bf16[128,2304]{1,0:T(8,128)(2,1)S(1)} %fusion.refs_0_, bf16[128,2304]{1,0:T(8,128)(2,1)S(1)} %collective-permute-done.2.refs_1_, bf16[128,2304]{1,0:T(8,128)(2,1)S(1)} %collective-permute-done.1.refs_2_, bf16[128,2304]{1,0:T(8,128)(2,1)S(1)} %collective-permute-done.refs_3_, ...), custom_call_target="tpu_custom_call" | custom-call | flops 5435817984 | bytes 12386304 | tf_op jit(solution)/shard_map/weight_times/pallas_call | solution.py:182
  84.1 0.5 slice.140
  84.6 0.8 add_convert_fusion.1
  85.4 4.7 %collective-permute-start.22 = (bf16[64,1152]{1,0:T(8,128)(2,1)S(1)}, bf16[64,1152]{1,0:T(8,128)(2,1)S(1)}, u32[]{:S(2)}, u32[]{:S(2)}) collective-permute-start(bf16[64,1152]{1,0:T(8,128)(2,1)S(1)} %get-tuple-element.77), channel_id=1, source_target_pairs={{0,130},{1,131},{2,132},{3,133},{4,134},{5,135},{6,136},{7,137},{8... | collective-permute-start | bytes 442376 | tf_op jit(solution)/shard_map/ppermute | solution.py:39
  90.1 2.3 %collective-permute-start.23 = (bf16[64,1152]{1,0:T(8,128)(2,1)S(1)}, bf16[64,1152]{1,0:T(8,128)(2,1)S(1)}, u32[]{:S(2)}, u32[]{:S(2)}) collective-permute-start(bf16[64,1152]{1,0:T(8,128)(2,1)S(1)} %get-tuple-element.78), channel_id=1, source_target_pairs={{0,131},{1,130},{2,133},{3,132},{4,135},{5,134},{6,137},{7,136},{8... | collective-permute-start | bytes 442376 | tf_op jit(solution)/shard_map/ppermute | solution.py:39
  92.4 2.9 %collective-permute-start.24 = (bf16[64,1152]{1,0:T(8,128)(2,1)S(1)}, bf16[64,1152]{1,0:T(8,128)(2,1)S(1)}, u32[]{:S(2)}, u32[]{:S(2)}) collective-permute-start(bf16[64,1152]{1,0:T(8,128)(2,1)S(1)} %get-tuple-element.79), channel_id=1, source_target_pairs={{0,142},{1,143},{2,128},{3,129},{4,130},{5,131},{6,132},{7,133},{8... | collective-permute-start | bytes 442376 | tf_op jit(solution)/shard_map/ppermute | solution.py:39
  95.3 3.0 %collective-permute-start.25 = (bf16[64,1152]{1,0:T(8,128)(2,1)S(1)}, bf16[64,1152]{1,0:T(8,128)(2,1)S(1)}, u32[]{:S(2)}, u32[]{:S(2)}) collective-permute-start(bf16[64,1152]{1,0:T(8,128)(2,1)S(1)} %get-tuple-element.80), channel_id=1, source_target_pairs={{0,143},{1,142},{2,129},{3,128},{4,131},{5,130},{6,133},{7,132},{8... | collective-permute-start | bytes 442376 | tf_op jit(solution)/shard_map/ppermute | solution.py:39
  98.3 7.2 %collective-permute-done.23 = bf16[64,1152]{1,0:T(8,128)(2,1)S(1)} collective-permute-done((bf16[64,1152]{1,0:T(8,128)(2,1)S(1)}, bf16[64,1152]{1,0:T(8,128)(2,1)S(1)}, u32[]{:S(2)}, u32[]{:S(2)}) %collective-permute-start.23) | collective-permute-done | bytes 147488 | tf_op jit(solution)/shard_map/ppermute | solution.py:39
  105.5 0.3 collective-permute-done.25
  105.8 0.8 fusion.1
  (44 shorter events, 0.6 us)
Async XLA Ops:
  0.6 6.2 %copy-start = (bf16[1,64,1152]{2,1,0:T(8,128)(2,1)S(1)}, bf16[1,64,1152]{2,1,0:T(8,128)(2,1)}, u32[]{:S(2)}) copy-start(bf16[1,64,1152]{2,1,0:T(8,128)(2,1)} %param.4) | copy-start | bytes 442372
  2.1 16.1 %collective-permute-start.2 = (bf16[128,2304]{1,0:T(8,128)(2,1)S(1)}, bf16[128,2304]{1,0:T(8,128)(2,1)S(1)}, u32[]{:S(2)}, u32[]{:S(2)}) collective-permute-start(bf16[128,2304]{1,0:T(8,128)(2,1)S(1)} %fusion.refs_0_), channel_id=1, source_target_pairs={{0,16},{16,0},{32,48},{48,32},{64,80},{80,64},{96,112},{112,96},{1... | collective-permute-start | bytes 1769480 | tf_op jit(solution)/shard_map/ppermute | solution.py:21
  4.3 14.2 %collective-permute-start.1 = (bf16[128,2304]{1,0:T(8,128)(2,1)S(1)}, bf16[128,2304]{1,0:T(8,128)(2,1)S(1)}, u32[]{:S(2)}, u32[]{:S(2)}) collective-permute-start(bf16[128,2304]{1,0:T(8,128)(2,1)S(1)} %fusion.refs_0_), channel_id=1, source_target_pairs={{0,96},{16,112},{32,0},{48,16},{64,32},{80,48},{96,64},{112,80},{1... | collective-permute-start | bytes 1769480 | tf_op jit(solution)/shard_map/ppermute | solution.py:16
  6.8 14.8 %collective-permute-start = (bf16[128,2304]{1,0:T(8,128)(2,1)S(1)}, bf16[128,2304]{1,0:T(8,128)(2,1)S(1)}, u32[]{:S(2)}, u32[]{:S(2)}) collective-permute-start(bf16[128,2304]{1,0:T(8,128)(2,1)S(1)} %fusion.refs_0_), channel_id=1, source_target_pairs={{0,32},{16,48},{32,64},{48,80},{64,96},{80,112},{96,0},{112,16},{1... | collective-permute-start | bytes 1769480 | tf_op jit(solution)/shard_map/ppermute | solution.py:16
  6.8 7.7 %collective-permute-start.6 = (bf16[64,1152]{1,0:T(8,128)(2,1)S(1)}, bf16[64,1152]{1,0:T(8,128)(2,1)S(1)}, u32[]{:S(2)}, u32[]{:S(2)}) collective-permute-start(bf16[64,1152]{1,0:T(8,128)(2,1)S(1)} %bitcast.13), channel_id=1, source_target_pairs={{0,2},{1,3},{2,4},{3,5},{4,6},{5,7},{6,8},{7,9},{8,10},{9,11},{10,... | collective-permute-start | bytes 442376 | tf_op jit(solution)/shard_map/ppermute | solution.py:30
  14.5 12.9 %collective-permute-start.8 = (bf16[128,1152]{1,0:T(8,128)(2,1)S(1)}, bf16[128,1152]{1,0:T(8,128)(2,1)S(1)}, u32[]{:S(2)}, u32[]{:S(2)}) collective-permute-start(bf16[128,1152]{1,0:T(8,128)(2,1)S(1)} %pad_maximum_fusion.8.refs_9_), channel_id=1, source_target_pairs={{0,12},{1,13},{2,14},{3,15},{4,0},{5,1},{6,2},{7,3},{8,4},{9,5},{1... | collective-permute-start | bytes 884744 | tf_op jit(solution)/shard_map/ppermute | solution.py:30
  14.6 17.6 %collective-permute-start.7 = (bf16[128,1152]{1,0:T(8,128)(2,1)S(1)}, bf16[128,1152]{1,0:T(8,128)(2,1)S(1)}, u32[]{:S(2)}, u32[]{:S(2)}) collective-permute-start(bf16[128,1152]{1,0:T(8,128)(2,1)S(1)} %pad_maximum_fusion.8.refs_9_), channel_id=1, source_target_pairs={{0,4},{1,5},{2,6},{3,7},{4,8},{5,9},{6,10},{7,11},{8,12},{9,13},{1... | collective-permute-start | bytes 884744 | tf_op jit(solution)/shard_map/ppermute | solution.py:30
  21.6 2.2 %slice-start = ((s8[5308416]{0:T(1024)(128)(4,1)}), s8[4194304]{0:T(1024)(128)(4,1)S(1)}, s32[]{:S(2)}) async-start(s8[5308416]{0:T(1024)(128)(4,1)} %bitcast.8), calls=%async_computation | async-start | bytes 8388608
  21.7 2.4 %slice-start.1 = ((s8[5308416]{0:T(1024)(128)(4,1)}), s8[1114112]{0:T(1024)(128)(4,1)S(1)}, s32[]{:S(2)}) async-start(s8[5308416]{0:T(1024)(128)(4,1)} %bitcast.8), calls=%async_computation.1 | async-start | bytes 2228224
  21.9 16.4 %collective-permute-start.5 = (bf16[128,2304]{1,0:T(8,128)(2,1)S(1)}, bf16[128,2304]{1,0:T(8,128)(2,1)S(1)}, u32[]{:S(2)}, u32[]{:S(2)}) collective-permute-start(bf16[128,2304]{1,0:T(8,128)(2,1)S(1)} %get-tuple-element.83), channel_id=1, source_target_pairs={{0,16},{16,0},{32,48},{48,32},{64,80},{80,64},{96,112},{112,96},{1... | collective-permute-start | bytes 1769480 | tf_op jit(solution)/shard_map/ppermute | solution.py:21
  22.1 16.1 %collective-permute-start.4 = (bf16[128,2304]{1,0:T(8,128)(2,1)S(1)}, bf16[128,2304]{1,0:T(8,128)(2,1)S(1)}, u32[]{:S(2)}, u32[]{:S(2)}) collective-permute-start(bf16[128,2304]{1,0:T(8,128)(2,1)S(1)} %get-tuple-element.84), channel_id=1, source_target_pairs={{0,96},{16,112},{32,0},{48,16},{64,32},{80,48},{96,64},{112,80},{1... | collective-permute-start | bytes 1769480 | tf_op jit(solution)/shard_map/ppermute | solution.py:16
  22.4 15.8 %collective-permute-start.3 = (bf16[128,2304]{1,0:T(8,128)(2,1)S(1)}, bf16[128,2304]{1,0:T(8,128)(2,1)S(1)}, u32[]{:S(2)}, u32[]{:S(2)}) collective-permute-start(bf16[128,2304]{1,0:T(8,128)(2,1)S(1)} %get-tuple-element.85), channel_id=1, source_target_pairs={{0,32},{16,48},{32,64},{48,80},{64,96},{80,112},{96,0},{112,16},{1... | collective-permute-start | bytes 1769480 | tf_op jit(solution)/shard_map/ppermute | solution.py:16
  27.4 10.8 %collective-permute-start.9 = (bf16[128,1152]{1,0:T(8,128)(2,1)S(1)}, bf16[128,1152]{1,0:T(8,128)(2,1)S(1)}, u32[]{:S(2)}, u32[]{:S(2)}) collective-permute-start(bf16[128,1152]{1,0:T(8,128)(2,1)S(1)} %collective-permute-done.8.refs_12_), channel_id=1, source_target_pairs={{0,12},{1,13},{2,14},{3,15},{4,0},{5,1},{6,2},{7,3},{8,4},{9,5},{1... | collective-permute-start | bytes 884744 | tf_op jit(solution)/shard_map/ppermute | solution.py:30
  38.5 7.1 %collective-permute-start.11 = (bf16[128,1152]{1,0:T(8,128)(2,1)S(1)}, bf16[128,1152]{1,0:T(8,128)(2,1)S(1)}, u32[]{:S(2)}, u32[]{:S(2)}) collective-permute-start(bf16[128,1152]{1,0:T(8,128)(2,1)S(1)} %pad_maximum_fusion.6), channel_id=1, source_target_pairs={{0,96},{16,112},{32,0},{48,16},{64,32},{80,48},{96,64},{112,80},{1... | collective-permute-start | bytes 884744 | tf_op jit(solution)/shard_map/ppermute | solution.py:16
  39.7 7.0 %collective-permute-start.10 = (bf16[128,1152]{1,0:T(8,128)(2,1)S(1)}, bf16[128,1152]{1,0:T(8,128)(2,1)S(1)}, u32[]{:S(2)}, u32[]{:S(2)}) collective-permute-start(bf16[128,1152]{1,0:T(8,128)(2,1)S(1)} %pad_maximum_fusion.7), channel_id=1, source_target_pairs={{0,32},{16,48},{32,64},{48,80},{64,96},{80,112},{96,0},{112,16},{1... | collective-permute-start | bytes 884744 | tf_op jit(solution)/shard_map/ppermute | solution.py:16
  42.9 18.8 %collective-permute-start.12 = (bf16[256,1152]{1,0:T(8,128)(2,1)S(1)}, bf16[256,1152]{1,0:T(8,128)(2,1)S(1)}, u32[]{:S(2)}, u32[]{:S(2)}) collective-permute-start(bf16[256,1152]{1,0:T(8,128)(2,1)S(1)} %pad_maximum_fusion.4), channel_id=1, source_target_pairs={{0,1},{1,0},{2,3},{3,2},{4,5},{5,4},{6,7},{7,6},{8,9},{9,8},{10,11... | collective-permute-start | bytes 1769480 | tf_op jit(solution)/shard_map/ppermute | solution.py:21
  48.8 7.7 %collective-permute-start.14 = (bf16[64,1152]{1,0:T(8,128)(2,1)S(1)}, bf16[64,1152]{1,0:T(8,128)(2,1)S(1)}, u32[]{:S(2)}, u32[]{:S(2)}) collective-permute-start(bf16[64,1152]{1,0:T(8,128)(2,1)S(1)} %get-tuple-element.64), channel_id=1, source_target_pairs={{0,14},{1,15},{2,0},{3,1},{4,2},{5,3},{6,4},{7,5},{8,6},{9,7},{10,... | collective-permute-start | bytes 442376 | tf_op jit(solution)/shard_map/ppermute | solution.py:16
  53.2 5.5 %collective-permute-start.13 = (bf16[64,1152]{1,0:T(8,128)(2,1)S(1)}, bf16[64,1152]{1,0:T(8,128)(2,1)S(1)}, u32[]{:S(2)}, u32[]{:S(2)}) collective-permute-start(bf16[64,1152]{1,0:T(8,128)(2,1)S(1)} %get-tuple-element.65), channel_id=1, source_target_pairs={{0,2},{1,3},{2,4},{3,5},{4,6},{5,7},{6,8},{7,9},{8,10},{9,11},{10,... | collective-permute-start | bytes 442376 | tf_op jit(solution)/shard_map/ppermute | solution.py:16
  53.3 21.1 %collective-permute-start.17 = (bf16[256,1152]{1,0:T(8,128)(2,1)S(1)}, bf16[256,1152]{1,0:T(8,128)(2,1)S(1)}, u32[]{:S(2)}, u32[]{:S(2)}) collective-permute-start(bf16[256,1152]{1,0:T(8,128)(2,1)S(1)} %pad_maximum_fusion.5), channel_id=1, source_target_pairs={{0,1},{1,0},{2,3},{3,2},{4,5},{5,4},{6,7},{7,6},{8,9},{9,8},{10,11... | collective-permute-start | bytes 1769480 | tf_op jit(solution)/shard_map/ppermute | solution.py:21
  58.9 15.6 %collective-permute-start.15 = (bf16[128,1152]{1,0:T(8,128)(2,1)S(1)}, bf16[128,1152]{1,0:T(8,128)(2,1)S(1)}, u32[]{:S(2)}, u32[]{:S(2)}) collective-permute-start(bf16[128,1152]{1,0:T(8,128)(2,1)S(1)} %pad_maximum_fusion.9), channel_id=1, source_target_pairs={{0,2},{1,3},{2,4},{3,5},{4,6},{5,7},{6,8},{7,9},{8,10},{9,11},{10,... | collective-permute-start | bytes 884744 | tf_op jit(solution)/shard_map/ppermute | solution.py:16
  59.0 15.4 %collective-permute-start.16 = (bf16[128,1152]{1,0:T(8,128)(2,1)S(1)}, bf16[128,1152]{1,0:T(8,128)(2,1)S(1)}, u32[]{:S(2)}, u32[]{:S(2)}) collective-permute-start(bf16[128,1152]{1,0:T(8,128)(2,1)S(1)} %pad_maximum_fusion.10), channel_id=1, source_target_pairs={{0,14},{1,15},{2,0},{3,1},{4,2},{5,3},{6,4},{7,5},{8,6},{9,7},{10,... | collective-permute-start | bytes 884744 | tf_op jit(solution)/shard_map/ppermute | solution.py:16
  61.7 22.3 %collective-permute-start.21 = (bf16[64,1152]{1,0:T(8,128)(2,1)S(1)}, bf16[64,1152]{1,0:T(8,128)(2,1)S(1)}, u32[]{:S(2)}, u32[]{:S(2)}) collective-permute-start(bf16[64,1152]{1,0:T(8,128)(2,1)S(1)} %get-tuple-element.81), channel_id=1, source_target_pairs={{0,129},{1,128},{2,131},{3,130},{4,133},{5,132},{6,135},{7,134},{8... | collective-permute-start | bytes 442376 | tf_op jit(solution)/shard_map/ppermute | solution.py:39
  74.4 9.6 %collective-permute-start.20 = (bf16[64,1152]{1,0:T(8,128)(2,1)S(1)}, bf16[64,1152]{1,0:T(8,128)(2,1)S(1)}, u32[]{:S(2)}, u32[]{:S(2)}) collective-permute-start(bf16[64,1152]{1,0:T(8,128)(2,1)S(1)} %get-tuple-element.82), channel_id=1, source_target_pairs={{0,128},{1,129},{2,130},{3,131},{4,132},{5,133},{6,134},{7,135},{8... | collective-permute-start | bytes 442376 | tf_op jit(solution)/shard_map/ppermute | solution.py:39
  74.6 9.4 %collective-permute-start.19 = (bf16[128,1152]{1,0:T(8,128)(2,1)S(1)}, bf16[128,1152]{1,0:T(8,128)(2,1)S(1)}, u32[]{:S(2)}, u32[]{:S(2)}) collective-permute-start(bf16[128,1152]{1,0:T(8,128)(2,1)S(1)} %get-tuple-element.60), channel_id=1, source_target_pairs={{0,14},{1,15},{2,0},{3,1},{4,2},{5,3},{6,4},{7,5},{8,6},{9,7},{10,... | collective-permute-start | bytes 884744 | tf_op jit(solution)/shard_map/ppermute | solution.py:16
  74.7 9.4 %collective-permute-start.18 = (bf16[128,1152]{1,0:T(8,128)(2,1)S(1)}, bf16[128,1152]{1,0:T(8,128)(2,1)S(1)}, u32[]{:S(2)}, u32[]{:S(2)}) collective-permute-start(bf16[128,1152]{1,0:T(8,128)(2,1)S(1)} %get-tuple-element.61), channel_id=1, source_target_pairs={{0,2},{1,3},{2,4},{3,5},{4,6},{5,7},{6,8},{7,9},{8,10},{9,11},{10,... | collective-permute-start | bytes 884744 | tf_op jit(solution)/shard_map/ppermute | solution.py:16
  85.4 12.9 %collective-permute-start.22 = (bf16[64,1152]{1,0:T(8,128)(2,1)S(1)}, bf16[64,1152]{1,0:T(8,128)(2,1)S(1)}, u32[]{:S(2)}, u32[]{:S(2)}) collective-permute-start(bf16[64,1152]{1,0:T(8,128)(2,1)S(1)} %get-tuple-element.77), channel_id=1, source_target_pairs={{0,130},{1,131},{2,132},{3,133},{4,134},{5,135},{6,136},{7,137},{8... | collective-permute-start | bytes 442376 | tf_op jit(solution)/shard_map/ppermute | solution.py:39
  90.1 15.5 %collective-permute-start.23 = (bf16[64,1152]{1,0:T(8,128)(2,1)S(1)}, bf16[64,1152]{1,0:T(8,128)(2,1)S(1)}, u32[]{:S(2)}, u32[]{:S(2)}) collective-permute-start(bf16[64,1152]{1,0:T(8,128)(2,1)S(1)} %get-tuple-element.78), channel_id=1, source_target_pairs={{0,131},{1,130},{2,133},{3,132},{4,135},{5,134},{6,137},{7,136},{8... | collective-permute-start | bytes 442376 | tf_op jit(solution)/shard_map/ppermute | solution.py:39
  92.4 13.2 %collective-permute-start.24 = (bf16[64,1152]{1,0:T(8,128)(2,1)S(1)}, bf16[64,1152]{1,0:T(8,128)(2,1)S(1)}, u32[]{:S(2)}, u32[]{:S(2)}) collective-permute-start(bf16[64,1152]{1,0:T(8,128)(2,1)S(1)} %get-tuple-element.79), channel_id=1, source_target_pairs={{0,142},{1,143},{2,128},{3,129},{4,130},{5,131},{6,132},{7,133},{8... | collective-permute-start | bytes 442376 | tf_op jit(solution)/shard_map/ppermute | solution.py:39
  95.3 10.5 %collective-permute-start.25 = (bf16[64,1152]{1,0:T(8,128)(2,1)S(1)}, bf16[64,1152]{1,0:T(8,128)(2,1)S(1)}, u32[]{:S(2)}, u32[]{:S(2)}) collective-permute-start(bf16[64,1152]{1,0:T(8,128)(2,1)S(1)} %get-tuple-element.80), channel_id=1, source_target_pairs={{0,143},{1,142},{2,129},{3,128},{4,131},{5,130},{6,133},{7,132},{8... | collective-permute-start | bytes 442376 | tf_op jit(solution)/shard_map/ppermute | solution.py:39

commit v3 on v2

--- a/solution.py
+++ b/solution.py
@@ -128,8 +128,8 @@
 
 
 def weight_kernel(*refs):
-    blocks, pieces = refs[:9], refs[9:15]
-    out_ref, token_ref, grads, inputs = refs[15:]
+    blocks, pieces = refs[:9], refs[9:16]
+    out_ref, grads, inputs = refs[16:]
     own, beside, right, left, from_left, from_right, from_beside, far_left, far_right = blocks
     half = own.shape[0] // 2
     middle = far_left.shape[1]
@@ -139,11 +139,11 @@
     def _():
         tensor, section = lax.axis_index("tensor"), lax.axis_index("section")
         z, y_hi = tensor // 2, tensor % 2
-        token_ref[...] = jnp.zeros_like(token_ref)
 
         def fill(spot, high, source, part, columns=slice(None)):
             apart = z - place(*(FIRST + SECOND + FAR)[spot])
             order = (apart * (1 - 2 * section) + Z) % Z
+            order ^= order // 4 * 2
             away = y_hi if high == 0 else 1 - y_hi
             where = pl.multiple_of((order + away * Z) * half, half)
             grads[pl.ds(where, half), columns] = source[part * half : (part + 1) * half, :]
@@ -183,14 +183,8 @@
         weight_kernel,
         grid=(wide // step,),
         in_specs=[pl.BlockSpec(memory_space=pltpu.VMEM)] * (len(blocks) + len(inputs)),
-        out_specs=(
-            pl.BlockSpec((step, depth), lambda i: (i, 0)),
-            pl.BlockSpec((8, 128), lambda i: (0, 0)),
-        ),
-        out_shape=(
-            jax.ShapeDtypeStruct((wide, depth), BF16),
-            jax.ShapeDtypeStruct((8, 128), F32),
-        ),
+        out_specs=pl.BlockSpec((step, depth), lambda i: (i, 0)),
+        out_shape=jax.ShapeDtypeStruct((wide, depth), BF16),
         scratch_shapes=[
             pltpu.VMEM((rows, depth), BF16),
             pltpu.VMEM((rows, wide), BF16),
@@ -234,8 +228,8 @@
     last, first_part = together((last, first_part))
     beyond = along_z(last, -2)
 
-    from_left, from_right, from_beside, near, beyond = together(
-        (from_left, from_right, from_beside, near, beyond)
+    from_left, from_right, from_beside, near = together(
+        (from_left, from_right, from_beside, near)
     )
     across = jnp.concatenate([from_left[:half], from_right[:half]])
     left_beside = jnp.concatenate([from_left[half:], from_beside[:half]])
@@ -243,13 +237,15 @@
     far_left = shift(left_beside[:, :middle], "dp", 2)
     far_right = shift(right_beside[:, middle:], "dp", -2)
 
-    second_part = times(jnp.concatenate([right_beside, across, left_beside]), weight)
+    second = jnp.concatenate([right_beside, across, left_beside])
+    second, beyond = together((second, beyond))
+    second_part = times(second, weight)
     held, second_part = together((held, second_part))
-    held_away = swap(jnp.concatenate([held, near]), "tensor")
+    held_away = swap(held, "tensor")
 
     terms = all_terms(first_part, second_part, far_left, far_right, weight)
-    beyond, terms = together((beyond, terms))
-    beyond_away = swap(jnp.concatenate([beyond, last]), "tensor")
+    near, terms = together((near, terms))
+    middle_away = swap(jnp.concatenate([near, last]), "tensor")
 
     def term(step):
         begin = step % Z * rows
@@ -262,29 +258,31 @@
         return jnp.concatenate([same, away])
 
     up, down = along(term(4)[:half], 1), along(term(4)[half:], -1)
-    up, down = together((up, down))
+    up, down, held_away, beyond, own_term = together(
+        (up, down, held_away, beyond, term(0).astype(BF16))
+    )
+    beyond_away = swap(beyond, "tensor")
 
     up, down = up.astype(F32), down.astype(F32)
     up = both(term(3)[:half] + up, term(3)[half:])
     down = both(term(-3)[:half], term(-3)[half:] + down)
     up, down = along(up, 1), along(down, -1)
-    held_away, own_term = together((held_away, term(0).astype(BF16)))
     pieces = [deliver(own_term[:half], 0, 0), deliver(own_term[half:], 0, 1)]
-    up, down, beyond_away = together((up, down, beyond_away))
-
-    up = along(term(2) + up.astype(F32), 1)
-    down = along(term(-2) + down.astype(F32), -1)
-    weight_grad, zeros = weight_times(
+    up, down, middle_away = together((up, down, middle_away))
+
+    up, down = term(2) + up.astype(F32), term(-2) + down.astype(F32)
+    parts = [(along(up[half:], 1), 1, half, 1), (along(down[half:], -1), -1, half, 1)]
+    parts += [(along(up[:half], 1), 1, 0, 0), (along(down[:half], -1), -1, 0, 0)]
+    arrived, *pieces = together((parts[0][0], *pieces))
+    parts[0] = (arrived, *parts[0][1:])
+    for part, dz, low, flip in parts:
+        total = term(dz)[low : low + half] + part.astype(F32)
+        pieces.append(deliver(total.astype(BF16), dz, flip))
+    handed = sum(piece.astype(F32) for piece in pieces).astype(BF16)
+    weight_grad = weight_times(
         (own, beside, right, left, from_left, from_right, from_beside, far_left, far_right),
-        (held, near, beyond, last, held_away, beyond_away),
+        (held, near, last, beyond, held_away, middle_away, beyond_away),
     )
-    up, down, zeros, *pieces = together((up, down, zeros, *pieces))
-    up, down = up.astype(F32) + zeros[:1, :1], down.astype(F32)
-
-    for total, dz in ((term(1) + up, 1), (term(-1) + down, -1)):
-        total = total.astype(BF16)
-        pieces += [deliver(total[:half], dz, 0), deliver(total[half:], dz, 1)]
-    handed = sum(piece.astype(F32) for piece in pieces).astype(BF16)
     return (weight_grad[None], handed[None])
 
 

time: 107 us -> 97.5 us (0.911)
  waiting for transfers between devices: 24.3 us -> 19.9 us
  starting transfers between devices: 60.8 us -> 56.6 us
    ppermute x4, waiting for transfers between devices: 9.84 us -> 3.92 us  [along_z(): return lax.ppermute(blocks, ('section', 'tensor'), route)]
    ppermute x6, starting transfers between devices: 25.6 us -> 20.9 us  [deliver(): return lax.ppermute(block, ('section', 'tensor'), route)]
    ppermute x6, waiting for transfers between devices: 7.48 us -> 3.67 us  [deliver(): return lax.ppermute(block, ('section', 'tensor'), route)]
    ppermute x12 -> x14, waiting for transfers between devices: 6.92 us -> 9.93 us  [shift(): lax.ppermute(block, axis, [(i, (i + distance) % n) for i in range(n)])]
    ppermute x4 -> x5, waiting for transfers between devices: 0.01 us -> 2.41 us  [swap(): return lax.ppermute(block, axis, [(i, i ^ 1) for i in range(n)])]
    ppermute x4 -> x5, starting transfers between devices: 8.32 us -> 8.61 us  [swap(): return lax.ppermute(block, axis, [(i, i ^ 1) for i in range(n)])]
    ppermute x12 -> x14, starting transfers between devices: 14.6 us -> 14.8 us  [shift(): lax.ppermute(block, axis, [(i, (i + distance) % n) for i in range(n)])]
  transfers between devices with their start and end apart: 26 -> 29, of which waited for: 9 -> 12; matrix products, arithmetic and copies ran while one was open for 1% -> 1% of each run, Pallas kernels for 15% -> 16%
where the time goes in v3:
time: 97.5 us; the launch traced here: 96.9 us
  starting transfers between devices  56.6 us (58%)
  waiting for transfers between devices  19.9 us (20%)
  Pallas kernels  15.5 us (16%)
  other arithmetic  3.12 us (3%)
    ppermute x6, starting transfers between devices, deliver(): return lax.ppermute(block, ('section', 'tensor'), route)  20.9 us
    ppermute x14, starting transfers between devices, shift(): lax.ppermute(block, axis, [(i, (i + distance) % n) for i in range(n)])  14.8 us
    ppermute x4, starting transfers between devices, along_z(): return lax.ppermute(blocks, ('section', 'tensor'), route)  12.3 us
    ppermute x14, waiting for transfers between devices, shift(): lax.ppermute(block, axis, [(i, (i + distance) % n) for i in range(n)])  9.93 us
    ppermute x5, starting transfers between devices, swap(): return lax.ppermute(block, axis, [(i, i ^ 1) for i in range(n)])  8.61 us
    pallas_call x1, Pallas kernels, weight_times(): pl.pallas_call(weight_kernel, grid=(wide // step,), in_specs=[pl.BlockSpe...  7.88 us
    pallas_call x2, Pallas kernels, times(): pl.pallas_call(times_kernel, in_specs=[pl.BlockSpec(memory_space=pltpu.VM...  5.71 us
    ppermute x4, waiting for transfers between devices, along_z(): return lax.ppermute(blocks, ('section', 'tensor'), route)  3.92 us
  transfers between devices with their start and end apart: 29, of which 12 were waited for; matrix products, arithmetic and copies ran while one was open for 1% of the time, Pallas kernels for 16%

profile of v3, /device:TPU:1, one launch (start us, length us, event | category | flops | bytes accessed | tf_op | source)
XLA Modules:
  0.0 96.9 jit_solution(8567432435535249288)
XLA Ops:
  0.6 1.5 %fusion.refs_0_ = bf16[128,2304]{1,0:T(8,128)(2,1)S(1)} fusion(bf16[1,128,2304]{2,1,0:T(8,128)(2,1)} %param.7, bf16[1,128,2304]{2,1,0:T(8,128)(2,1)} %param.6), kind=kLoop, calls=%fused_computation.4 | loop fusion | flops 1769472 | bytes 1769472 | tf_op jit(solution)/shard_map/mul | solution.py:212
  2.1 2.2 %collective-permute-start.2 = (bf16[128,2304]{1,0:T(8,128)(2,1)S(1)}, bf16[128,2304]{1,0:T(8,128)(2,1)S(1)}, u32[]{:S(2)}, u32[]{:S(2)}) collective-permute-start(bf16[128,2304]{1,0:T(8,128)(2,1)S(1)} %fusion.refs_0_), channel_id=1, source_target_pairs={{0,16},{16,0},{32,48},{48,32},{64,80},{80,64},{96,112},{112,96},{1... | collective-permute-start | bytes 1769480 | tf_op jit(solution)/shard_map/ppermute | solution.py:21
  4.3 2.5 %collective-permute-start.1 = (bf16[128,2304]{1,0:T(8,128)(2,1)S(1)}, bf16[128,2304]{1,0:T(8,128)(2,1)S(1)}, u32[]{:S(2)}, u32[]{:S(2)}) collective-permute-start(bf16[128,2304]{1,0:T(8,128)(2,1)S(1)} %fusion.refs_0_), channel_id=1, source_target_pairs={{0,96},{16,112},{32,0},{48,16},{64,32},{80,48},{96,64},{112,80},{1... | collective-permute-start | bytes 1769480 | tf_op jit(solution)/shard_map/ppermute | solution.py:16
  6.8 5.6 %collective-permute-start.6 = (bf16[64,1152]{1,0:T(8,128)(2,1)S(1)}, bf16[64,1152]{1,0:T(8,128)(2,1)S(1)}, u32[]{:S(2)}, u32[]{:S(2)}) collective-permute-start(bf16[64,1152]{1,0:T(8,128)(2,1)S(1)} %bitcast.12), channel_id=1, source_target_pairs={{0,2},{1,3},{2,4},{3,5},{4,6},{5,7},{6,8},{7,9},{8,10},{9,11},{10,... | collective-permute-start | bytes 442376 | tf_op jit(solution)/shard_map/ppermute | solution.py:30
  12.4 2.1 %collective-permute-done.6 = bf16[64,1152]{1,0:T(8,128)(2,1)S(1)} collective-permute-done((bf16[64,1152]{1,0:T(8,128)(2,1)S(1)}, bf16[64,1152]{1,0:T(8,128)(2,1)S(1)}, u32[]{:S(2)}, u32[]{:S(2)}) %collective-permute-start.6) | collective-permute-done | bytes 147488 | tf_op jit(solution)/shard_map/ppermute | solution.py:30
  14.5 0.1 collective-permute-start.10
  14.6 3.6 %collective-permute-start.7 = (bf16[128,1152]{1,0:T(8,128)(2,1)S(1)}, bf16[128,1152]{1,0:T(8,128)(2,1)S(1)}, u32[]{:S(2)}, u32[]{:S(2)}) collective-permute-start(bf16[128,1152]{1,0:T(8,128)(2,1)S(1)} %pad_maximum_fusion.7.refs_9_), channel_id=1, source_target_pairs={{0,4},{1,5},{2,6},{3,7},{4,8},{5,9},{6,10},{7,11},{8,12},{9,13},{1... | collective-permute-start | bytes 884744 | tf_op jit(solution)/shard_map/ppermute | solution.py:30
  18.2 0.3 collective-permute-done.1.refs_2_
  18.5 3.1 %collective-permute-done.refs_3_ = bf16[128,2304]{1,0:T(8,128)(2,1)S(1)} collective-permute-done((bf16[128,2304]{1,0:T(8,128)(2,1)S(1)}, bf16[128,2304]{1,0:T(8,128)(2,1)S(1)}, u32[]{:S(2)}, u32[]{:S(2)}) %collective-permute-start) | collective-permute-done | bytes 589856 | tf_op jit(solution)/shard_map/ppermute | solution.py:16
  21.7 0.1 pad_maximum_fusion.3
  21.9 0.3 collective-permute-start.5
  22.1 0.3 collective-permute-start.4
  22.4 1.2 %collective-permute-start.3 = (bf16[128,2304]{1,0:T(8,128)(2,1)S(1)}, bf16[128,2304]{1,0:T(8,128)(2,1)S(1)}, u32[]{:S(2)}, u32[]{:S(2)}) collective-permute-start(bf16[128,2304]{1,0:T(8,128)(2,1)S(1)} %get-tuple-element.86), channel_id=1, source_target_pairs={{0,32},{16,48},{32,64},{48,80},{64,96},{80,112},{96,0},{112,16},{1... | collective-permute-start | bytes 1769480 | tf_op jit(solution)/shard_map/ppermute | solution.py:16
  23.6 0.2 pad_maximum_fusion.block_ref
  23.8 0.3 slice-done.1
  24.2 3.2 %times.2.first_ref = bf16[512,1152]{1,0:T(8,128)(2,1)S(1)} custom-call(bf16[512,2304]{1,0:T(8,128)(2,1)S(1)} %pad_maximum_fusion.block_ref, bf16[1152,2304]{1,0:T(8,128)(2,1)S(1)} %bitcast.9), custom_call_target="tpu_custom_call" | custom-call | flops 2717908992 | bytes 8847360 | tf_op jit(solution)/shard_map/times/pallas_call | solution.py:57
  27.4 3.1 %collective-permute-start.11 = (bf16[128,1152]{1,0:T(8,128)(2,1)S(1)}, bf16[128,1152]{1,0:T(8,128)(2,1)S(1)}, u32[]{:S(2)}, u32[]{:S(2)}) collective-permute-start(bf16[128,1152]{1,0:T(8,128)(2,1)S(1)} %collective-permute-done.10.refs_11_), channel_id=1, source_target_pairs={{0,12},{1,13},{2,14},{3,15},{4,0},{5,1},{6,2},{7,3},{8,4},{9,5},{1... | collective-permute-start | bytes 884744 | tf_op jit(solution)/shard_map/ppermute | solution.py:30
  30.5 1.7 %collective-permute-done.7.refs_10_ = bf16[128,1152]{1,0:T(8,128)(2,1)S(1)} collective-permute-done((bf16[128,1152]{1,0:T(8,128)(2,1)S(1)}, bf16[128,1152]{1,0:T(8,128)(2,1)S(1)}, u32[]{:S(2)}, u32[]{:S(2)}) %collective-permute-start.7) | collective-permute-done | bytes 294944 | tf_op jit(solution)/shard_map/ppermute | solution.py:30
  32.2 2.4 %collective-permute-done.5.refs_6_ = bf16[128,2304]{1,0:T(8,128)(2,1)S(1)} collective-permute-done((bf16[128,2304]{1,0:T(8,128)(2,1)S(1)}, bf16[128,2304]{1,0:T(8,128)(2,1)S(1)}, u32[]{:S(2)}, u32[]{:S(2)}) %collective-permute-start.5) | collective-permute-done | bytes 589856 | tf_op jit(solution)/shard_map/ppermute | solution.py:21
  34.6 1.4 %collective-permute-done.3.refs_4_ = bf16[128,2304]{1,0:T(8,128)(2,1)S(1)} collective-permute-done((bf16[128,2304]{1,0:T(8,128)(2,1)S(1)}, bf16[128,2304]{1,0:T(8,128)(2,1)S(1)}, u32[]{:S(2)}, u32[]{:S(2)}) %collective-permute-start.3) | collective-permute-done | bytes 589856 | tf_op jit(solution)/shard_map/ppermute | solution.py:16
  36.3 0.4 collective-permute-start.9
  36.7 1.4 %collective-permute-start.8 = (bf16[128,1152]{1,0:T(8,128)(2,1)S(1)}, bf16[128,1152]{1,0:T(8,128)(2,1)S(1)}, u32[]{:S(2)}, u32[]{:S(2)}) collective-permute-start(bf16[128,1152]{1,0:T(8,128)(2,1)S(1)} %pad_maximum_fusion.6), channel_id=1, source_target_pairs={{0,32},{16,48},{32,64},{48,80},{64,96},{80,112},{96,0},{112,16},{1... | collective-permute-start | bytes 884744 | tf_op jit(solution)/shard_map/ppermute | solution.py:16
  38.1 0.1 collective-permute-done.11.refs_12_
  38.2 2.5 %times.3.second_ref = bf16[384,1152]{1,0:T(8,128)(2,1)S(1)} custom-call(bf16[384,2304]{1,0:T(8,128)(2,1)S(1)} %get-tuple-element.35.block_ref, bf16[1152,2304]{1,0:T(8,128)(2,1)S(1)} %bitcast.10), custom_call_target="tpu_custom_call" | custom-call | flops 2038431744 | bytes 7962624 | tf_op jit(solution)/shard_map/times/pallas_call | solution.py:57
  40.7 2.9 %collective-permute-start.14 = (bf16[128,1152]{1,0:T(8,128)(2,1)S(1)}, bf16[128,1152]{1,0:T(8,128)(2,1)S(1)}, u32[]{:S(2)}, u32[]{:S(2)}) collective-permute-start(bf16[128,1152]{1,0:T(8,128)(2,1)S(1)} %pad_maximum_fusion.7.refs_9_), channel_id=1, source_target_pairs={{0,1},{1,0},{2,3},{3,2},{4,5},{5,4},{6,7},{7,6},{8,9},{9,8},{10,11... | collective-permute-start | bytes 884744 | tf_op jit(solution)/shard_map/ppermute | solution.py:21
  43.6 0.1 collective-permute-done.8.left_ref.refs_7_
  43.7 1.9 %all_terms.1 = bf16[1024,1152]{1,0:T(8,128)(2,1)S(1)} custom-call(bf16[512,1152]{1,0:T(8,128)(2,1)S(1)} %times.2.first_ref, bf16[384,1152]{1,0:T(8,128)(2,1)S(1)} %times.3.second_ref, bf16[128,1152]{1,0:T(8,128)(2,1)S(1)} %collective-permute-done.8.left_ref.refs_7_, bf16[128,1152]{1,0:T(8,128)(2,1)S(1)} %collective-permute-done.9.right_ref.refs_8_, ...), custom_call_target="tpu_custom_call" | custom-call | flops 679477248 | bytes 10616832 | tf_op jit(solution)/shard_map/all_terms/pallas_call | solution.py:115
  45.6 0.1 slice_convert_fusion.1
  45.8 5.7 %collective-permute-start.13 = (bf16[64,1152]{1,0:T(8,128)(2,1)S(1)}, bf16[64,1152]{1,0:T(8,128)(2,1)S(1)}, u32[]{:S(2)}, u32[]{:S(2)}) collective-permute-start(bf16[64,1152]{1,0:T(8,128)(2,1)S(1)} %get-tuple-element.61), channel_id=1, source_target_pairs={{0,14},{1,15},{2,0},{3,1},{4,2},{5,3},{6,4},{7,5},{8,6},{9,7},{10,... | collective-permute-start | bytes 442376 | tf_op jit(solution)/shard_map/ppermute | solution.py:16
  51.5 3.0 %collective-permute-start.17 = (bf16[256,1152]{1,0:T(8,128)(2,1)S(1)}, bf16[256,1152]{1,0:T(8,128)(2,1)S(1)}, u32[]{:S(2)}, u32[]{:S(2)}) collective-permute-start(bf16[256,1152]{1,0:T(8,128)(2,1)S(1)} %pad_maximum_fusion.4), channel_id=1, source_target_pairs={{0,1},{1,0},{2,3},{3,2},{4,5},{5,4},{6,7},{7,6},{8,9},{9,8},{10,11... | collective-permute-start | bytes 1769480 | tf_op jit(solution)/shard_map/ppermute | solution.py:21
  54.5 2.1 %collective-permute-done.12 = bf16[64,1152]{1,0:T(8,128)(2,1)S(1)} collective-permute-done((bf16[64,1152]{1,0:T(8,128)(2,1)S(1)}, bf16[64,1152]{1,0:T(8,128)(2,1)S(1)}, u32[]{:S(2)}, u32[]{:S(2)}) %collective-permute-start.12) | collective-permute-done | bytes 147488 | tf_op jit(solution)/shard_map/ppermute | solution.py:16
  56.7 0.1 add_convert_fusion.3
  56.8 0.1 collective-permute-start.15
  56.9 2.7 %collective-permute-start.16 = (bf16[128,1152]{1,0:T(8,128)(2,1)S(1)}, bf16[128,1152]{1,0:T(8,128)(2,1)S(1)}, u32[]{:S(2)}, u32[]{:S(2)}) collective-permute-start(bf16[128,1152]{1,0:T(8,128)(2,1)S(1)} %pad_maximum_fusion.9), channel_id=1, source_target_pairs={{0,14},{1,15},{2,0},{3,1},{4,2},{5,3},{6,4},{7,5},{8,6},{9,7},{10,... | collective-permute-start | bytes 884744 | tf_op jit(solution)/shard_map/ppermute | solution.py:16
  59.6 10.8 %collective-permute-start.21 = (bf16[64,1152]{1,0:T(8,128)(2,1)S(1)}, bf16[64,1152]{1,0:T(8,128)(2,1)S(1)}, u32[]{:S(2)}, u32[]{:S(2)}) collective-permute-start(bf16[64,1152]{1,0:T(8,128)(2,1)S(1)} %get-tuple-element.78), channel_id=1, source_target_pairs={{0,129},{1,128},{2,131},{3,130},{4,133},{5,132},{6,135},{7,134},{8... | collective-permute-start | bytes 442376 | tf_op jit(solution)/shard_map/ppermute | solution.py:39
  70.5 0.2 collective-permute-start.18
  70.7 0.1 add_convert_fusion.1
  70.9 0.1 collective-permute-start.19
  70.9 0.1 collective-permute-start.25
  71.1 3.7 %collective-permute-done.21 = bf16[64,1152]{1,0:T(8,128)(2,1)S(1)} collective-permute-done((bf16[64,1152]{1,0:T(8,128)(2,1)S(1)}, bf16[64,1152]{1,0:T(8,128)(2,1)S(1)}, u32[]{:S(2)}, u32[]{:S(2)}) %collective-permute-start.21) | collective-permute-done | bytes 147488 | tf_op jit(solution)/shard_map/ppermute | solution.py:39
  74.7 0.5 collective-permute-start.27
  75.2 0.9 collective-permute-done.19
  76.1 1.9 %collective-permute-done.25 = bf16[64,1152]{1,0:T(8,128)(2,1)S(1)} collective-permute-done((bf16[64,1152]{1,0:T(8,128)(2,1)S(1)}, bf16[64,1152]{1,0:T(8,128)(2,1)S(1)}, u32[]{:S(2)}, u32[]{:S(2)}) %collective-permute-start.25) | collective-permute-done | bytes 147488 | tf_op jit(solution)/shard_map/ppermute | solution.py:16
  78.1 5.0 %collective-permute-start.22 = (bf16[64,1152]{1,0:T(8,128)(2,1)S(1)}, bf16[64,1152]{1,0:T(8,128)(2,1)S(1)}, u32[]{:S(2)}, u32[]{:S(2)}) collective-permute-start(bf16[64,1152]{1,0:T(8,128)(2,1)S(1)} %get-tuple-element.65), channel_id=1, source_target_pairs={{0,131},{1,130},{2,133},{3,132},{4,135},{5,134},{6,137},{7,136},{8... | collective-permute-start | bytes 442376 | tf_op jit(solution)/shard_map/ppermute | solution.py:39
  83.1 4.6 %collective-permute-start.24 = (bf16[64,1152]{1,0:T(8,128)(2,1)S(1)}, bf16[64,1152]{1,0:T(8,128)(2,1)S(1)}, u32[]{:S(2)}, u32[]{:S(2)}) collective-permute-start(bf16[64,1152]{1,0:T(8,128)(2,1)S(1)} %get-tuple-element.67), channel_id=1, source_target_pairs={{0,143},{1,142},{2,129},{3,128},{4,131},{5,130},{6,133},{7,132},{8... | collective-permute-start | bytes 442376 | tf_op jit(solution)/shard_map/ppermute | solution.py:39
  87.8 0.5 collective-permute-start.28
  88.2 7.9 %weight_times.1 = bf16[1152,2304]{1,0:T(8,128)(2,1)} custom-call(bf16[128,2304]{1,0:T(8,128)(2,1)S(1)} %fusion.refs_0_, bf16[128,2304]{1,0:T(8,128)(2,1)S(1)} %collective-permute-done.2.refs_1_, bf16[128,2304]{1,0:T(8,128)(2,1)S(1)} %collective-permute-done.1.refs_2_, bf16[128,2304]{1,0:T(8,128)(2,1)S(1)} %collective-permute-done.refs_3_, ...), custom_call_target="tpu_custom_call" | custom-call | flops 5435817984 | bytes 12386304 | tf_op jit(solution)/shard_map/weight_times/pallas_call | solution.py:182
  96.1 0.8 fusion.5
  (49 shorter events, 0.8 us)
Async XLA Ops:
  0.6 6.2 %copy-start = (bf16[1,64,1152]{2,1,0:T(8,128)(2,1)S(1)}, bf16[1,64,1152]{2,1,0:T(8,128)(2,1)}, u32[]{:S(2)}) copy-start(bf16[1,64,1152]{2,1,0:T(8,128)(2,1)} %param.4) | copy-start | bytes 442372
  2.1 16.1 %collective-permute-start.2 = (bf16[128,2304]{1,0:T(8,128)(2,1)S(1)}, bf16[128,2304]{1,0:T(8,128)(2,1)S(1)}, u32[]{:S(2)}, u32[]{:S(2)}) collective-permute-start(bf16[128,2304]{1,0:T(8,128)(2,1)S(1)} %fusion.refs_0_), channel_id=1, source_target_pairs={{0,16},{16,0},{32,48},{48,32},{64,80},{80,64},{96,112},{112,96},{1... | collective-permute-start | bytes 1769480 | tf_op jit(solution)/shard_map/ppermute | solution.py:21
  4.3 14.2 %collective-permute-start.1 = (bf16[128,2304]{1,0:T(8,128)(2,1)S(1)}, bf16[128,2304]{1,0:T(8,128)(2,1)S(1)}, u32[]{:S(2)}, u32[]{:S(2)}) collective-permute-start(bf16[128,2304]{1,0:T(8,128)(2,1)S(1)} %fusion.refs_0_), channel_id=1, source_target_pairs={{0,96},{16,112},{32,0},{48,16},{64,32},{80,48},{96,64},{112,80},{1... | collective-permute-start | bytes 1769480 | tf_op jit(solution)/shard_map/ppermute | solution.py:16
  6.8 14.8 %collective-permute-start = (bf16[128,2304]{1,0:T(8,128)(2,1)S(1)}, bf16[128,2304]{1,0:T(8,128)(2,1)S(1)}, u32[]{:S(2)}, u32[]{:S(2)}) collective-permute-start(bf16[128,2304]{1,0:T(8,128)(2,1)S(1)} %fusion.refs_0_), channel_id=1, source_target_pairs={{0,32},{16,48},{32,64},{48,80},{64,96},{80,112},{96,0},{112,16},{1... | collective-permute-start | bytes 1769480 | tf_op jit(solution)/shard_map/ppermute | solution.py:16
  6.8 7.7 %collective-permute-start.6 = (bf16[64,1152]{1,0:T(8,128)(2,1)S(1)}, bf16[64,1152]{1,0:T(8,128)(2,1)S(1)}, u32[]{:S(2)}, u32[]{:S(2)}) collective-permute-start(bf16[64,1152]{1,0:T(8,128)(2,1)S(1)} %bitcast.12), channel_id=1, source_target_pairs={{0,2},{1,3},{2,4},{3,5},{4,6},{5,7},{6,8},{7,9},{8,10},{9,11},{10,... | collective-permute-start | bytes 442376 | tf_op jit(solution)/shard_map/ppermute | solution.py:30
  14.5 12.9 %collective-permute-start.10 = (bf16[128,1152]{1,0:T(8,128)(2,1)S(1)}, bf16[128,1152]{1,0:T(8,128)(2,1)S(1)}, u32[]{:S(2)}, u32[]{:S(2)}) collective-permute-start(bf16[128,1152]{1,0:T(8,128)(2,1)S(1)} %pad_maximum_fusion.7.refs_9_), channel_id=1, source_target_pairs={{0,12},{1,13},{2,14},{3,15},{4,0},{5,1},{6,2},{7,3},{8,4},{9,5},{1... | collective-permute-start | bytes 884744 | tf_op jit(solution)/shard_map/ppermute | solution.py:30
  14.6 17.6 %collective-permute-start.7 = (bf16[128,1152]{1,0:T(8,128)(2,1)S(1)}, bf16[128,1152]{1,0:T(8,128)(2,1)S(1)}, u32[]{:S(2)}, u32[]{:S(2)}) collective-permute-start(bf16[128,1152]{1,0:T(8,128)(2,1)S(1)} %pad_maximum_fusion.7.refs_9_), channel_id=1, source_target_pairs={{0,4},{1,5},{2,6},{3,7},{4,8},{5,9},{6,10},{7,11},{8,12},{9,13},{1... | collective-permute-start | bytes 884744 | tf_op jit(solution)/shard_map/ppermute | solution.py:30
  21.6 2.2 %slice-start = ((s8[5308416]{0:T(1024)(128)(4,1)}), s8[4194304]{0:T(1024)(128)(4,1)S(1)}, s32[]{:S(2)}) async-start(s8[5308416]{0:T(1024)(128)(4,1)} %bitcast.7), calls=%async_computation | async-start | bytes 8388608
  21.7 2.4 %slice-start.1 = ((s8[5308416]{0:T(1024)(128)(4,1)}), s8[1114112]{0:T(1024)(128)(4,1)S(1)}, s32[]{:S(2)}) async-start(s8[5308416]{0:T(1024)(128)(4,1)} %bitcast.7), calls=%async_computation.1 | async-start | bytes 2228224
  21.9 12.7 %collective-permute-start.5 = (bf16[128,2304]{1,0:T(8,128)(2,1)S(1)}, bf16[128,2304]{1,0:T(8,128)(2,1)S(1)}, u32[]{:S(2)}, u32[]{:S(2)}) collective-permute-start(bf16[128,2304]{1,0:T(8,128)(2,1)S(1)} %get-tuple-element.84), channel_id=1, source_target_pairs={{0,16},{16,0},{32,48},{48,32},{64,80},{80,64},{96,112},{112,96},{1... | collective-permute-start | bytes 1769480 | tf_op jit(solution)/shard_map/ppermute | solution.py:21
  22.1 12.5 %collective-permute-start.4 = (bf16[128,2304]{1,0:T(8,128)(2,1)S(1)}, bf16[128,2304]{1,0:T(8,128)(2,1)S(1)}, u32[]{:S(2)}, u32[]{:S(2)}) collective-permute-start(bf16[128,2304]{1,0:T(8,128)(2,1)S(1)} %get-tuple-element.85), channel_id=1, source_target_pairs={{0,96},{16,112},{32,0},{48,16},{64,32},{80,48},{96,64},{112,80},{1... | collective-permute-start | bytes 1769480 | tf_op jit(solution)/shard_map/ppermute | solution.py:16
  22.4 13.6 %collective-permute-start.3 = (bf16[128,2304]{1,0:T(8,128)(2,1)S(1)}, bf16[128,2304]{1,0:T(8,128)(2,1)S(1)}, u32[]{:S(2)}, u32[]{:S(2)}) collective-permute-start(bf16[128,2304]{1,0:T(8,128)(2,1)S(1)} %get-tuple-element.86), channel_id=1, source_target_pairs={{0,32},{16,48},{32,64},{48,80},{64,96},{80,112},{96,0},{112,16},{1... | collective-permute-start | bytes 1769480 | tf_op jit(solution)/shard_map/ppermute | solution.py:16
  27.4 10.8 %collective-permute-start.11 = (bf16[128,1152]{1,0:T(8,128)(2,1)S(1)}, bf16[128,1152]{1,0:T(8,128)(2,1)S(1)}, u32[]{:S(2)}, u32[]{:S(2)}) collective-permute-start(bf16[128,1152]{1,0:T(8,128)(2,1)S(1)} %collective-permute-done.10.refs_11_), channel_id=1, source_target_pairs={{0,12},{1,13},{2,14},{3,15},{4,0},{5,1},{6,2},{7,3},{8,4},{9,5},{1... | collective-permute-start | bytes 884744 | tf_op jit(solution)/shard_map/ppermute | solution.py:30
  36.3 7.3 %collective-permute-start.9 = (bf16[128,1152]{1,0:T(8,128)(2,1)S(1)}, bf16[128,1152]{1,0:T(8,128)(2,1)S(1)}, u32[]{:S(2)}, u32[]{:S(2)}) collective-permute-start(bf16[128,1152]{1,0:T(8,128)(2,1)S(1)} %pad_maximum_fusion.5), channel_id=1, source_target_pairs={{0,96},{16,112},{32,0},{48,16},{64,32},{80,48},{96,64},{112,80},{1... | collective-permute-start | bytes 884744 | tf_op jit(solution)/shard_map/ppermute | solution.py:16
  36.7 7.0 %collective-permute-start.8 = (bf16[128,1152]{1,0:T(8,128)(2,1)S(1)}, bf16[128,1152]{1,0:T(8,128)(2,1)S(1)}, u32[]{:S(2)}, u32[]{:S(2)}) collective-permute-start(bf16[128,1152]{1,0:T(8,128)(2,1)S(1)} %pad_maximum_fusion.6), channel_id=1, source_target_pairs={{0,32},{16,48},{32,64},{48,80},{64,96},{80,112},{96,0},{112,16},{1... | collective-permute-start | bytes 884744 | tf_op jit(solution)/shard_map/ppermute | solution.py:16
  40.7 13.8 %collective-permute-start.14 = (bf16[128,1152]{1,0:T(8,128)(2,1)S(1)}, bf16[128,1152]{1,0:T(8,128)(2,1)S(1)}, u32[]{:S(2)}, u32[]{:S(2)}) collective-permute-start(bf16[128,1152]{1,0:T(8,128)(2,1)S(1)} %pad_maximum_fusion.7.refs_9_), channel_id=1, source_target_pairs={{0,1},{1,0},{2,3},{3,2},{4,5},{5,4},{6,7},{7,6},{8,9},{9,8},{10,11... | collective-permute-start | bytes 884744 | tf_op jit(solution)/shard_map/ppermute | solution.py:21
  45.8 8.7 %collective-permute-start.13 = (bf16[64,1152]{1,0:T(8,128)(2,1)S(1)}, bf16[64,1152]{1,0:T(8,128)(2,1)S(1)}, u32[]{:S(2)}, u32[]{:S(2)}) collective-permute-start(bf16[64,1152]{1,0:T(8,128)(2,1)S(1)} %get-tuple-element.61), channel_id=1, source_target_pairs={{0,14},{1,15},{2,0},{3,1},{4,2},{5,3},{6,4},{7,5},{8,6},{9,7},{10,... | collective-permute-start | bytes 442376 | tf_op jit(solution)/shard_map/ppermute | solution.py:16
  51.4 5.2 %collective-permute-start.12 = (bf16[64,1152]{1,0:T(8,128)(2,1)S(1)}, bf16[64,1152]{1,0:T(8,128)(2,1)S(1)}, u32[]{:S(2)}, u32[]{:S(2)}) collective-permute-start(bf16[64,1152]{1,0:T(8,128)(2,1)S(1)} %get-tuple-element.62), channel_id=1, source_target_pairs={{0,2},{1,3},{2,4},{3,5},{4,6},{5,7},{6,8},{7,9},{8,10},{9,11},{10,... | collective-permute-start | bytes 442376 | tf_op jit(solution)/shard_map/ppermute | solution.py:16
  51.5 19.2 %collective-permute-start.17 = (bf16[256,1152]{1,0:T(8,128)(2,1)S(1)}, bf16[256,1152]{1,0:T(8,128)(2,1)S(1)}, u32[]{:S(2)}, u32[]{:S(2)}) collective-permute-start(bf16[256,1152]{1,0:T(8,128)(2,1)S(1)} %pad_maximum_fusion.4), channel_id=1, source_target_pairs={{0,1},{1,0},{2,3},{3,2},{4,5},{5,4},{6,7},{7,6},{8,9},{9,8},{10,11... | collective-permute-start | bytes 1769480 | tf_op jit(solution)/shard_map/ppermute | solution.py:21
  56.8 13.7 %collective-permute-start.15 = (bf16[128,1152]{1,0:T(8,128)(2,1)S(1)}, bf16[128,1152]{1,0:T(8,128)(2,1)S(1)}, u32[]{:S(2)}, u32[]{:S(2)}) collective-permute-start(bf16[128,1152]{1,0:T(8,128)(2,1)S(1)} %pad_maximum_fusion.8), channel_id=1, source_target_pairs={{0,2},{1,3},{2,4},{3,5},{4,6},{5,7},{6,8},{7,9},{8,10},{9,11},{10,... | collective-permute-start | bytes 884744 | tf_op jit(solution)/shard_map/ppermute | solution.py:16
  56.9 13.8 %collective-permute-start.16 = (bf16[128,1152]{1,0:T(8,128)(2,1)S(1)}, bf16[128,1152]{1,0:T(8,128)(2,1)S(1)}, u32[]{:S(2)}, u32[]{:S(2)}) collective-permute-start(bf16[128,1152]{1,0:T(8,128)(2,1)S(1)} %pad_maximum_fusion.9), channel_id=1, source_target_pairs={{0,14},{1,15},{2,0},{3,1},{4,2},{5,3},{6,4},{7,5},{8,6},{9,7},{10,... | collective-permute-start | bytes 884744 | tf_op jit(solution)/shard_map/ppermute | solution.py:16
  59.6 15.1 %collective-permute-start.21 = (bf16[64,1152]{1,0:T(8,128)(2,1)S(1)}, bf16[64,1152]{1,0:T(8,128)(2,1)S(1)}, u32[]{:S(2)}, u32[]{:S(2)}) collective-permute-start(bf16[64,1152]{1,0:T(8,128)(2,1)S(1)} %get-tuple-element.78), channel_id=1, source_target_pairs={{0,129},{1,128},{2,131},{3,130},{4,133},{5,132},{6,135},{7,134},{8... | collective-permute-start | bytes 442376 | tf_op jit(solution)/shard_map/ppermute | solution.py:39
  70.5 4.3 %collective-permute-start.20 = (bf16[64,1152]{1,0:T(8,128)(2,1)S(1)}, bf16[64,1152]{1,0:T(8,128)(2,1)S(1)}, u32[]{:S(2)}, u32[]{:S(2)}) collective-permute-start(bf16[64,1152]{1,0:T(8,128)(2,1)S(1)} %get-tuple-element.79), channel_id=1, source_target_pairs={{0,128},{1,129},{2,130},{3,131},{4,132},{5,133},{6,134},{7,135},{8... | collective-permute-start | bytes 442376 | tf_op jit(solution)/shard_map/ppermute | solution.py:39
  70.5 17.8 %collective-permute-start.18 = (bf16[128,1152]{1,0:T(8,128)(2,1)S(1)}, bf16[128,1152]{1,0:T(8,128)(2,1)S(1)}, u32[]{:S(2)}, u32[]{:S(2)}) collective-permute-start(bf16[128,1152]{1,0:T(8,128)(2,1)S(1)} %collective-permute-done.11.refs_12_), channel_id=1, source_target_pairs={{0,1},{1,0},{2,3},{3,2},{4,5},{5,4},{6,7},{7,6},{8,9},{9,8},{10,11... | collective-permute-start | bytes 884744 | tf_op jit(solution)/shard_map/ppermute | solution.py:21
  70.9 5.3 %collective-permute-start.19 = (bf16[64,1152]{1,0:T(8,128)(2,1)S(1)}, bf16[64,1152]{1,0:T(8,128)(2,1)S(1)}, u32[]{:S(2)}, u32[]{:S(2)}) collective-permute-start(bf16[64,1152]{1,0:T(8,128)(2,1)S(1)} %get-tuple-element.80), channel_id=1, source_target_pairs={{0,2},{1,3},{2,4},{3,5},{4,6},{5,7},{6,8},{7,9},{8,10},{9,11},{10,... | collective-permute-start | bytes 442376 | tf_op jit(solution)/shard_map/ppermute | solution.py:16
  70.9 7.1 %collective-permute-start.25 = (bf16[64,1152]{1,0:T(8,128)(2,1)S(1)}, bf16[64,1152]{1,0:T(8,128)(2,1)S(1)}, u32[]{:S(2)}, u32[]{:S(2)}) collective-permute-start(bf16[64,1152]{1,0:T(8,128)(2,1)S(1)} %get-tuple-element.81), channel_id=1, source_target_pairs={{0,2},{1,3},{2,4},{3,5},{4,6},{5,7},{6,8},{7,9},{8,10},{9,11},{10,... | collective-permute-start | bytes 442376 | tf_op jit(solution)/shard_map/ppermute | solution.py:16
  74.7 8.3 %collective-permute-start.23 = (bf16[64,1152]{1,0:T(8,128)(2,1)S(1)}, bf16[64,1152]{1,0:T(8,128)(2,1)S(1)}, u32[]{:S(2)}, u32[]{:S(2)}) collective-permute-start(bf16[64,1152]{1,0:T(8,128)(2,1)S(1)} %get-tuple-element.82), channel_id=1, source_target_pairs={{0,14},{1,15},{2,0},{3,1},{4,2},{5,3},{6,4},{7,5},{8,6},{9,7},{10,... | collective-permute-start | bytes 442376 | tf_op jit(solution)/shard_map/ppermute | solution.py:16
  74.7 8.3 %collective-permute-start.27 = (bf16[64,1152]{1,0:T(8,128)(2,1)S(1)}, bf16[64,1152]{1,0:T(8,128)(2,1)S(1)}, u32[]{:S(2)}, u32[]{:S(2)}) collective-permute-start(bf16[64,1152]{1,0:T(8,128)(2,1)S(1)} %get-tuple-element.83), channel_id=1, source_target_pairs={{0,14},{1,15},{2,0},{3,1},{4,2},{5,3},{6,4},{7,5},{8,6},{9,7},{10,... | collective-permute-start | bytes 442376 | tf_op jit(solution)/shard_map/ppermute | solution.py:16
  78.1 18.0 %collective-permute-start.22 = (bf16[64,1152]{1,0:T(8,128)(2,1)S(1)}, bf16[64,1152]{1,0:T(8,128)(2,1)S(1)}, u32[]{:S(2)}, u32[]{:S(2)}) collective-permute-start(bf16[64,1152]{1,0:T(8,128)(2,1)S(1)} %get-tuple-element.65), channel_id=1, source_target_pairs={{0,131},{1,130},{2,133},{3,132},{4,135},{5,134},{6,137},{7,136},{8... | collective-permute-start | bytes 442376 | tf_op jit(solution)/shard_map/ppermute | solution.py:39
  83.1 13.0 %collective-permute-start.26 = (bf16[64,1152]{1,0:T(8,128)(2,1)S(1)}, bf16[64,1152]{1,0:T(8,128)(2,1)S(1)}, u32[]{:S(2)}, u32[]{:S(2)}) collective-permute-start(bf16[64,1152]{1,0:T(8,128)(2,1)S(1)} %get-tuple-element.66), channel_id=1, source_target_pairs={{0,130},{1,131},{2,132},{3,133},{4,134},{5,135},{6,136},{7,137},{8... | collective-permute-start | bytes 442376 | tf_op jit(solution)/shard_map/ppermute | solution.py:39
  83.1 13.0 %collective-permute-start.24 = (bf16[64,1152]{1,0:T(8,128)(2,1)S(1)}, bf16[64,1152]{1,0:T(8,128)(2,1)S(1)}, u32[]{:S(2)}, u32[]{:S(2)}) collective-permute-start(bf16[64,1152]{1,0:T(8,128)(2,1)S(1)} %get-tuple-element.67), channel_id=1, source_target_pairs={{0,143},{1,142},{2,129},{3,128},{4,131},{5,130},{6,133},{7,132},{8... | collective-permute-start | bytes 442376 | tf_op jit(solution)/shard_map/ppermute | solution.py:39
  87.8 8.4 %collective-permute-start.28 = (bf16[64,1152]{1,0:T(8,128)(2,1)S(1)}, bf16[64,1152]{1,0:T(8,128)(2,1)S(1)}, u32[]{:S(2)}, u32[]{:S(2)}) collective-permute-start(bf16[64,1152]{1,0:T(8,128)(2,1)S(1)} %get-tuple-element.68), channel_id=1, source_target_pairs={{0,142},{1,143},{2,128},{3,129},{4,130},{5,131},{6,132},{7,133},{8... | collective-permute-start | bytes 442376 | tf_op jit(solution)/shard_map/ppermute | solution.py:39

commit v4 on v3

--- a/solution.py
+++ b/solution.py
@@ -254,29 +254,32 @@
     def along(total, direction):
         return shift(total.astype(BF16), "tensor", 2 * direction)
 
-    def both(same, away):
-        return jnp.concatenate([same, away])
-
-    up, down = along(term(4)[:half], 1), along(term(4)[half:], -1)
-    up, down, held_away, beyond, own_term = together(
-        (up, down, held_away, beyond, term(0).astype(BF16))
-    )
+    def half_of(step, low, part=0.0):
+        return term(step)[low : low + half] + part
+
+    up_same, down_away = along(half_of(4, 0), 1), along(half_of(4, half), -1)
+    up_away, down_same = along(half_of(3, half), 1), along(half_of(-3, 0), -1)
+    up_same, down_away, up_away, down_same, held_away = together(
+        (up_same, down_away, up_away, down_same, held_away)
+    )
+    up_away = along(half_of(2, half, up_away.astype(F32)), 1)
+    down_same = along(half_of(-2, 0, down_same.astype(F32)), -1)
+    up_same = along(half_of(3, 0, up_same.astype(F32)), 1)
+    down_away = along(half_of(-3, half, down_away.astype(F32)), -1)
+    up_away, down_same, up_same, down_away, middle_away, beyond, own_term = together(
+        (up_away, down_same, up_same, down_away, middle_away, beyond, term(0).astype(BF16))
+    )
+    up_same = along(half_of(2, 0, up_same.astype(F32)), 1)
+    down_away = along(half_of(-2, half, down_away.astype(F32)), -1)
     beyond_away = swap(beyond, "tensor")
-
-    up, down = up.astype(F32), down.astype(F32)
-    up = both(term(3)[:half] + up, term(3)[half:])
-    down = both(term(-3)[:half], term(-3)[half:] + down)
-    up, down = along(up, 1), along(down, -1)
     pieces = [deliver(own_term[:half], 0, 0), deliver(own_term[half:], 0, 1)]
-    up, down, middle_away = together((up, down, middle_away))
-
-    up, down = term(2) + up.astype(F32), term(-2) + down.astype(F32)
-    parts = [(along(up[half:], 1), 1, half, 1), (along(down[half:], -1), -1, half, 1)]
-    parts += [(along(up[:half], 1), 1, 0, 0), (along(down[:half], -1), -1, 0, 0)]
-    arrived, *pieces = together((parts[0][0], *pieces))
-    parts[0] = (arrived, *parts[0][1:])
-    for part, dz, low, flip in parts:
-        total = term(dz)[low : low + half] + part.astype(F32)
+    for part, dz, low, flip in (
+        (up_away, 1, half, 1),
+        (down_same, -1, 0, 0),
+        (up_same, 1, 0, 0),
+        (down_away, -1, half, 1),
+    ):
+        total = half_of(dz, low, part.astype(F32))
         pieces.append(deliver(total.astype(BF16), dz, flip))
     handed = sum(piece.astype(F32) for piece in pieces).astype(BF16)
     weight_grad = weight_times(

time: 97.5 us -> 110 us (1.13)
  starting transfers between devices: 56.6 us -> 64.4 us
  waiting for transfers between devices: 19.9 us -> 25.4 us
    ppermute x5, waiting for transfers between devices: 2.41 us -> 9.69 us  [swap(): return lax.ppermute(block, axis, [(i, i ^ 1) for i in range(n)])]
    ppermute x14 -> x16, starting transfers between devices: 14.8 us -> 21.2 us  [shift(): lax.ppermute(block, axis, [(i, (i + distance) % n) for i in range(n)])]
    ppermute x6, waiting for transfers between devices: 3.67 us -> 0.02 us  [deliver(): return lax.ppermute(block, ('section', 'tensor'), route)]
    ppermute x14 -> x16, waiting for transfers between devices: 9.93 us -> 11.8 us  [shift(): lax.ppermute(block, axis, [(i, (i + distance) % n) for i in range(n)])]
    ppermute x6, starting transfers between devices: 20.9 us -> 22.5 us  [deliver(): return lax.ppermute(block, ('section', 'tensor'), route)]
  transfers between devices with their start and end apart: 29 -> 31, of which waited for: 12 -> 12; matrix products, arithmetic and copies ran while one was open for 1% -> 1% of each run, Pallas kernels for 16% -> 14%
where the time goes in v4:
time: 110 us
  starting transfers between devices  64.4 us (59%)
  waiting for transfers between devices  25.4 us (23%)
  Pallas kernels  15.5 us (14%)
  other arithmetic  3.18 us (3%)
    ppermute x6, starting transfers between devices, deliver(): return lax.ppermute(block, ('section', 'tensor'), route)  22.5 us
    ppermute x16, starting transfers between devices, shift(): lax.ppermute(block, axis, [(i, (i + distance) % n) for i in range(n)])  21.2 us
    ppermute x4, starting transfers between devices, along_z(): return lax.ppermute(blocks, ('section', 'tensor'), route)  12.3 us
    ppermute x16, waiting for transfers between devices, shift(): lax.ppermute(block, axis, [(i, (i + distance) % n) for i in range(n)])  11.8 us
    ppermute x5, waiting for transfers between devices, swap(): return lax.ppermute(block, axis, [(i, i ^ 1) for i in range(n)])  9.69 us
    ppermute x5, starting transfers between devices, swap(): return lax.ppermute(block, axis, [(i, i ^ 1) for i in range(n)])  8.46 us
    pallas_call x1, Pallas kernels, weight_times(): pl.pallas_call(weight_kernel, grid=(wide // step,), in_specs=[pl.BlockSpe...  7.88 us
    pallas_call x2, Pallas kernels, times(): pl.pallas_call(times_kernel, in_specs=[pl.BlockSpec(memory_space=pltpu.VM...  5.71 us
  transfers between devices with their start and end apart: 31, of which 12 were waited for; matrix products, arithmetic and copies ran while one was open for 1% of the time, Pallas kernels for 14%

profile of v4, /device:TPU:1, one launch (start us, length us, event | category | flops | bytes accessed | tf_op | source)
XLA Modules:
  0.0 110.1 jit_solution(15851540797104504548)
XLA Ops:
  0.6 1.5 %fusion.refs_0_ = bf16[128,2304]{1,0:T(8,128)(2,1)S(1)} fusion(bf16[1,128,2304]{2,1,0:T(8,128)(2,1)} %param.7, bf16[1,128,2304]{2,1,0:T(8,128)(2,1)} %param.6), kind=kLoop, calls=%fused_computation.4 | loop fusion | flops 1769472 | bytes 1769472 | tf_op jit(solution)/shard_map/mul | solution.py:212
  2.1 2.2 %collective-permute-start.2 = (bf16[128,2304]{1,0:T(8,128)(2,1)S(1)}, bf16[128,2304]{1,0:T(8,128)(2,1)S(1)}, u32[]{:S(2)}, u32[]{:S(2)}) collective-permute-start(bf16[128,2304]{1,0:T(8,128)(2,1)S(1)} %fusion.refs_0_), channel_id=1, source_target_pairs={{0,16},{16,0},{32,48},{48,32},{64,80},{80,64},{96,112},{112,96},{1... | collective-permute-start | bytes 1769480 | tf_op jit(solution)/shard_map/ppermute | solution.py:21
  4.3 2.5 %collective-permute-start.1 = (bf16[128,2304]{1,0:T(8,128)(2,1)S(1)}, bf16[128,2304]{1,0:T(8,128)(2,1)S(1)}, u32[]{:S(2)}, u32[]{:S(2)}) collective-permute-start(bf16[128,2304]{1,0:T(8,128)(2,1)S(1)} %fusion.refs_0_), channel_id=1, source_target_pairs={{0,96},{16,112},{32,0},{48,16},{64,32},{80,48},{96,64},{112,80},{1... | collective-permute-start | bytes 1769480 | tf_op jit(solution)/shard_map/ppermute | solution.py:16
  6.8 5.6 %collective-permute-start.6 = (bf16[64,1152]{1,0:T(8,128)(2,1)S(1)}, bf16[64,1152]{1,0:T(8,128)(2,1)S(1)}, u32[]{:S(2)}, u32[]{:S(2)}) collective-permute-start(bf16[64,1152]{1,0:T(8,128)(2,1)S(1)} %bitcast.12), channel_id=1, source_target_pairs={{0,2},{1,3},{2,4},{3,5},{4,6},{5,7},{6,8},{7,9},{8,10},{9,11},{10,... | collective-permute-start | bytes 442376 | tf_op jit(solution)/shard_map/ppermute | solution.py:30
  12.4 2.1 %collective-permute-done.6 = bf16[64,1152]{1,0:T(8,128)(2,1)S(1)} collective-permute-done((bf16[64,1152]{1,0:T(8,128)(2,1)S(1)}, bf16[64,1152]{1,0:T(8,128)(2,1)S(1)}, u32[]{:S(2)}, u32[]{:S(2)}) %collective-permute-start.6) | collective-permute-done | bytes 147488 | tf_op jit(solution)/shard_map/ppermute | solution.py:30
  14.5 0.1 collective-permute-start.10
  14.6 3.6 %collective-permute-start.7 = (bf16[128,1152]{1,0:T(8,128)(2,1)S(1)}, bf16[128,1152]{1,0:T(8,128)(2,1)S(1)}, u32[]{:S(2)}, u32[]{:S(2)}) collective-permute-start(bf16[128,1152]{1,0:T(8,128)(2,1)S(1)} %pad_maximum_fusion.7.refs_9_), channel_id=1, source_target_pairs={{0,4},{1,5},{2,6},{3,7},{4,8},{5,9},{6,10},{7,11},{8,12},{9,13},{1... | collective-permute-start | bytes 884744 | tf_op jit(solution)/shard_map/ppermute | solution.py:30
  18.2 0.3 collective-permute-done.1.refs_2_
  18.5 3.1 %collective-permute-done.refs_3_ = bf16[128,2304]{1,0:T(8,128)(2,1)S(1)} collective-permute-done((bf16[128,2304]{1,0:T(8,128)(2,1)S(1)}, bf16[128,2304]{1,0:T(8,128)(2,1)S(1)}, u32[]{:S(2)}, u32[]{:S(2)}) %collective-permute-start) | collective-permute-done | bytes 589856 | tf_op jit(solution)/shard_map/ppermute | solution.py:16
  21.7 0.1 pad_maximum_fusion.3
  21.9 0.3 collective-permute-start.5
  22.1 0.3 collective-permute-start.4
  22.4 1.2 %collective-permute-start.3 = (bf16[128,2304]{1,0:T(8,128)(2,1)S(1)}, bf16[128,2304]{1,0:T(8,128)(2,1)S(1)}, u32[]{:S(2)}, u32[]{:S(2)}) collective-permute-start(bf16[128,2304]{1,0:T(8,128)(2,1)S(1)} %get-tuple-element.84), channel_id=1, source_target_pairs={{0,32},{16,48},{32,64},{48,80},{64,96},{80,112},{96,0},{112,16},{1... | collective-permute-start | bytes 1769480 | tf_op jit(solution)/shard_map/ppermute | solution.py:16
  23.6 0.2 pad_maximum_fusion.block_ref
  23.8 0.3 slice-done.1
  24.2 3.2 %times.2.first_ref = bf16[512,1152]{1,0:T(8,128)(2,1)S(1)} custom-call(bf16[512,2304]{1,0:T(8,128)(2,1)S(1)} %pad_maximum_fusion.block_ref, bf16[1152,2304]{1,0:T(8,128)(2,1)S(1)} %bitcast.9), custom_call_target="tpu_custom_call" | custom-call | flops 2717908992 | bytes 8847360 | tf_op jit(solution)/shard_map/times/pallas_call | solution.py:57
  27.4 3.1 %collective-permute-start.11 = (bf16[128,1152]{1,0:T(8,128)(2,1)S(1)}, bf16[128,1152]{1,0:T(8,128)(2,1)S(1)}, u32[]{:S(2)}, u32[]{:S(2)}) collective-permute-start(bf16[128,1152]{1,0:T(8,128)(2,1)S(1)} %collective-permute-done.10.refs_11_), channel_id=1, source_target_pairs={{0,12},{1,13},{2,14},{3,15},{4,0},{5,1},{6,2},{7,3},{8,4},{9,5},{1... | collective-permute-start | bytes 884744 | tf_op jit(solution)/shard_map/ppermute | solution.py:30
  30.5 1.7 %collective-permute-done.7.refs_10_ = bf16[128,1152]{1,0:T(8,128)(2,1)S(1)} collective-permute-done((bf16[128,1152]{1,0:T(8,128)(2,1)S(1)}, bf16[128,1152]{1,0:T(8,128)(2,1)S(1)}, u32[]{:S(2)}, u32[]{:S(2)}) %collective-permute-start.7) | collective-permute-done | bytes 294944 | tf_op jit(solution)/shard_map/ppermute | solution.py:30
  32.2 2.4 %collective-permute-done.5.refs_6_ = bf16[128,2304]{1,0:T(8,128)(2,1)S(1)} collective-permute-done((bf16[128,2304]{1,0:T(8,128)(2,1)S(1)}, bf16[128,2304]{1,0:T(8,128)(2,1)S(1)}, u32[]{:S(2)}, u32[]{:S(2)}) %collective-permute-start.5) | collective-permute-done | bytes 589856 | tf_op jit(solution)/shard_map/ppermute | solution.py:21
  34.6 1.4 %collective-permute-done.3.refs_4_ = bf16[128,2304]{1,0:T(8,128)(2,1)S(1)} collective-permute-done((bf16[128,2304]{1,0:T(8,128)(2,1)S(1)}, bf16[128,2304]{1,0:T(8,128)(2,1)S(1)}, u32[]{:S(2)}, u32[]{:S(2)}) %collective-permute-start.3) | collective-permute-done | bytes 589856 | tf_op jit(solution)/shard_map/ppermute | solution.py:16
  36.3 0.4 collective-permute-start.9
  36.7 1.4 %collective-permute-start.8 = (bf16[128,1152]{1,0:T(8,128)(2,1)S(1)}, bf16[128,1152]{1,0:T(8,128)(2,1)S(1)}, u32[]{:S(2)}, u32[]{:S(2)}) collective-permute-start(bf16[128,1152]{1,0:T(8,128)(2,1)S(1)} %pad_maximum_fusion.6), channel_id=1, source_target_pairs={{0,32},{16,48},{32,64},{48,80},{64,96},{80,112},{96,0},{112,16},{1... | collective-permute-start | bytes 884744 | tf_op jit(solution)/shard_map/ppermute | solution.py:16
  38.2 2.5 %times.3.second_ref = bf16[384,1152]{1,0:T(8,128)(2,1)S(1)} custom-call(bf16[384,2304]{1,0:T(8,128)(2,1)S(1)} %get-tuple-element.36.block_ref, bf16[1152,2304]{1,0:T(8,128)(2,1)S(1)} %bitcast.10), custom_call_target="tpu_custom_call" | custom-call | flops 2038431744 | bytes 7962624 | tf_op jit(solution)/shard_map/times/pallas_call | solution.py:57
  40.7 2.9 %collective-permute-start.16 = (bf16[128,1152]{1,0:T(8,128)(2,1)S(1)}, bf16[128,1152]{1,0:T(8,128)(2,1)S(1)}, u32[]{:S(2)}, u32[]{:S(2)}) collective-permute-start(bf16[128,1152]{1,0:T(8,128)(2,1)S(1)} %pad_maximum_fusion.7.refs_9_), channel_id=1, source_target_pairs={{0,1},{1,0},{2,3},{3,2},{4,5},{5,4},{6,7},{7,6},{8,9},{9,8},{10,11... | collective-permute-start | bytes 884744 | tf_op jit(solution)/shard_map/ppermute | solution.py:21
  43.6 0.1 collective-permute-done.8.left_ref.refs_7_
  43.7 1.9 %all_terms.1 = bf16[1024,1152]{1,0:T(8,128)(2,1)S(1)} custom-call(bf16[512,1152]{1,0:T(8,128)(2,1)S(1)} %times.2.first_ref, bf16[384,1152]{1,0:T(8,128)(2,1)S(1)} %times.3.second_ref, bf16[128,1152]{1,0:T(8,128)(2,1)S(1)} %collective-permute-done.8.left_ref.refs_7_, bf16[128,1152]{1,0:T(8,128)(2,1)S(1)} %collective-permute-done.9.right_ref.refs_8_, ...), custom_call_target="tpu_custom_call" | custom-call | flops 679477248 | bytes 10616832 | tf_op jit(solution)/shard_map/all_terms/pallas_call | solution.py:115
  45.6 0.2 slice_convert_fusion.1
  45.9 5.7 %collective-permute-start.15 = (bf16[64,1152]{1,0:T(8,128)(2,1)S(1)}, bf16[64,1152]{1,0:T(8,128)(2,1)S(1)}, u32[]{:S(2)}, u32[]{:S(2)}) collective-permute-start(bf16[64,1152]{1,0:T(8,128)(2,1)S(1)} %get-tuple-element.63), channel_id=1, source_target_pairs={{0,14},{1,15},{2,0},{3,1},{4,2},{5,3},{6,4},{7,5},{8,6},{9,7},{10,... | collective-permute-start | bytes 442376 | tf_op jit(solution)/shard_map/ppermute | solution.py:16
  51.5 2.7 %collective-permute-start.13 = (bf16[64,1152]{1,0:T(8,128)(2,1)S(1)}, bf16[64,1152]{1,0:T(8,128)(2,1)S(1)}, u32[]{:S(2)}, u32[]{:S(2)}) collective-permute-start(bf16[64,1152]{1,0:T(8,128)(2,1)S(1)} %get-tuple-element.65), channel_id=1, source_target_pairs={{0,14},{1,15},{2,0},{3,1},{4,2},{5,3},{6,4},{7,5},{8,6},{9,7},{10,... | collective-permute-start | bytes 442376 | tf_op jit(solution)/shard_map/ppermute | solution.py:16
  54.2 3.0 %collective-permute-start.21 = (bf16[256,1152]{1,0:T(8,128)(2,1)S(1)}, bf16[256,1152]{1,0:T(8,128)(2,1)S(1)}, u32[]{:S(2)}, u32[]{:S(2)}) collective-permute-start(bf16[256,1152]{1,0:T(8,128)(2,1)S(1)} %pad_maximum_fusion.4), channel_id=1, source_target_pairs={{0,1},{1,0},{2,3},{3,2},{4,5},{5,4},{6,7},{7,6},{8,9},{9,8},{10,11... | collective-permute-start | bytes 1769480 | tf_op jit(solution)/shard_map/ppermute | solution.py:21
  57.3 2.1 %collective-permute-done.12 = bf16[64,1152]{1,0:T(8,128)(2,1)S(1)} collective-permute-done((bf16[64,1152]{1,0:T(8,128)(2,1)S(1)}, bf16[64,1152]{1,0:T(8,128)(2,1)S(1)}, u32[]{:S(2)}, u32[]{:S(2)}) %collective-permute-start.12) | collective-permute-done | bytes 147488 | tf_op jit(solution)/shard_map/ppermute | solution.py:16
  59.4 0.1 add_convert_fusion.1
  59.5 0.6 collective-permute-start.20
  60.1 0.9 collective-permute-start.19
  61.0 0.1 collective-permute-start.17
  61.2 2.7 %collective-permute-start.18 = (bf16[64,1152]{1,0:T(8,128)(2,1)S(1)}, bf16[64,1152]{1,0:T(8,128)(2,1)S(1)}, u32[]{:S(2)}, u32[]{:S(2)}) collective-permute-start(bf16[64,1152]{1,0:T(8,128)(2,1)S(1)} %fusion.7), channel_id=1, source_target_pairs={{0,14},{1,15},{2,0},{3,1},{4,2},{5,3},{6,4},{7,5},{8,6},{9,7},{10,... | collective-permute-start | bytes 442376 | tf_op jit(solution)/shard_map/ppermute | solution.py:16
  63.9 3.1 %collective-permute-done.19 = bf16[64,1152]{1,0:T(8,128)(2,1)S(1)} collective-permute-done((bf16[64,1152]{1,0:T(8,128)(2,1)S(1)}, bf16[64,1152]{1,0:T(8,128)(2,1)S(1)}, u32[]{:S(2)}, u32[]{:S(2)}) %collective-permute-start.19) | collective-permute-done | bytes 147488 | tf_op jit(solution)/shard_map/ppermute | solution.py:16
  67.1 1.6 %collective-permute-done.17 = bf16[64,1152]{1,0:T(8,128)(2,1)S(1)} collective-permute-done((bf16[64,1152]{1,0:T(8,128)(2,1)S(1)}, bf16[64,1152]{1,0:T(8,128)(2,1)S(1)}, u32[]{:S(2)}, u32[]{:S(2)}) %collective-permute-start.17) | collective-permute-done | bytes 147488 | tf_op jit(solution)/shard_map/ppermute | solution.py:16
  68.7 0.1 collective-permute-start.27
  68.8 2.7 %collective-permute-start.29 = (bf16[64,1152]{1,0:T(8,128)(2,1)S(1)}, bf16[64,1152]{1,0:T(8,128)(2,1)S(1)}, u32[]{:S(2)}, u32[]{:S(2)}) collective-permute-start(bf16[64,1152]{1,0:T(8,128)(2,1)S(1)} %fusion.1), channel_id=1, source_target_pairs={{0,14},{1,15},{2,0},{3,1},{4,2},{5,3},{6,4},{7,5},{8,6},{9,7},{10,... | collective-permute-start | bytes 442376 | tf_op jit(solution)/shard_map/ppermute | solution.py:16
  71.5 9.3 %collective-permute-start.23 = (bf16[64,1152]{1,0:T(8,128)(2,1)S(1)}, bf16[64,1152]{1,0:T(8,128)(2,1)S(1)}, u32[]{:S(2)}, u32[]{:S(2)}) collective-permute-start(bf16[64,1152]{1,0:T(8,128)(2,1)S(1)} %get-tuple-element.80), channel_id=1, source_target_pairs={{0,128},{1,129},{2,130},{3,131},{4,132},{5,133},{6,134},{7,135},{8... | collective-permute-start | bytes 442376 | tf_op jit(solution)/shard_map/ppermute | solution.py:39
  80.8 3.0 %collective-permute-start.24 = (bf16[64,1152]{1,0:T(8,128)(2,1)S(1)}, bf16[64,1152]{1,0:T(8,128)(2,1)S(1)}, u32[]{:S(2)}, u32[]{:S(2)}) collective-permute-start(bf16[64,1152]{1,0:T(8,128)(2,1)S(1)} %get-tuple-element.81), channel_id=1, source_target_pairs={{0,129},{1,128},{2,131},{3,130},{4,133},{5,132},{6,135},{7,134},{8... | collective-permute-start | bytes 442376 | tf_op jit(solution)/shard_map/ppermute | solution.py:39
  84.0 1.9 %collective-permute-start.25 = (bf16[64,1152]{1,0:T(8,128)(2,1)S(1)}, bf16[64,1152]{1,0:T(8,128)(2,1)S(1)}, u32[]{:S(2)}, u32[]{:S(2)}) collective-permute-start(bf16[64,1152]{1,0:T(8,128)(2,1)S(1)} %get-tuple-element.67), channel_id=1, source_target_pairs={{0,131},{1,130},{2,133},{3,132},{4,135},{5,134},{6,137},{7,136},{8... | collective-permute-start | bytes 442376 | tf_op jit(solution)/shard_map/ppermute | solution.py:39
  86.0 3.8 %collective-permute-start.26 = (bf16[64,1152]{1,0:T(8,128)(2,1)S(1)}, bf16[64,1152]{1,0:T(8,128)(2,1)S(1)}, u32[]{:S(2)}, u32[]{:S(2)}) collective-permute-start(bf16[64,1152]{1,0:T(8,128)(2,1)S(1)} %get-tuple-element.69), channel_id=1, source_target_pairs={{0,142},{1,143},{2,128},{3,129},{4,130},{5,131},{6,132},{7,133},{8... | collective-permute-start | bytes 442376 | tf_op jit(solution)/shard_map/ppermute | solution.py:39
  89.8 7.3 %collective-permute-done.22.refs_15_ = bf16[128,1152]{1,0:T(8,128)(2,1)S(1)} collective-permute-done((bf16[128,1152]{1,0:T(8,128)(2,1)S(1)}, bf16[128,1152]{1,0:T(8,128)(2,1)S(1)}, u32[]{:S(2)}, u32[]{:S(2)}) %collective-permute-start.22) | collective-permute-done | bytes 294944 | tf_op jit(solution)/shard_map/ppermute | solution.py:21
  97.1 4.4 %collective-permute-start.30 = (bf16[64,1152]{1,0:T(8,128)(2,1)S(1)}, bf16[64,1152]{1,0:T(8,128)(2,1)S(1)}, u32[]{:S(2)}, u32[]{:S(2)}) collective-permute-start(bf16[64,1152]{1,0:T(8,128)(2,1)S(1)} %get-tuple-element.70), channel_id=1, source_target_pairs={{0,143},{1,142},{2,129},{3,128},{4,131},{5,130},{6,133},{7,132},{8... | collective-permute-start | bytes 442376 | tf_op jit(solution)/shard_map/ppermute | solution.py:39
  101.4 7.9 %weight_times.1 = bf16[1152,2304]{1,0:T(8,128)(2,1)} custom-call(bf16[128,2304]{1,0:T(8,128)(2,1)S(1)} %fusion.refs_0_, bf16[128,2304]{1,0:T(8,128)(2,1)S(1)} %collective-permute-done.2.refs_1_, bf16[128,2304]{1,0:T(8,128)(2,1)S(1)} %collective-permute-done.1.refs_2_, bf16[128,2304]{1,0:T(8,128)(2,1)S(1)} %collective-permute-done.refs_3_, ...), custom_call_target="tpu_custom_call" | custom-call | flops 5435817984 | bytes 12386304 | tf_op jit(solution)/shard_map/weight_times/pallas_call | solution.py:182
  109.4 0.8 fusion.9
  (52 shorter events, 1.0 us)
Async XLA Ops:
  0.6 6.2 %copy-start = (bf16[1,64,1152]{2,1,0:T(8,128)(2,1)S(1)}, bf16[1,64,1152]{2,1,0:T(8,128)(2,1)}, u32[]{:S(2)}) copy-start(bf16[1,64,1152]{2,1,0:T(8,128)(2,1)} %param.4) | copy-start | bytes 442372
  2.1 16.1 %collective-permute-start.2 = (bf16[128,2304]{1,0:T(8,128)(2,1)S(1)}, bf16[128,2304]{1,0:T(8,128)(2,1)S(1)}, u32[]{:S(2)}, u32[]{:S(2)}) collective-permute-start(bf16[128,2304]{1,0:T(8,128)(2,1)S(1)} %fusion.refs_0_), channel_id=1, source_target_pairs={{0,16},{16,0},{32,48},{48,32},{64,80},{80,64},{96,112},{112,96},{1... | collective-permute-start | bytes 1769480 | tf_op jit(solution)/shard_map/ppermute | solution.py:21
  4.3 14.2 %collective-permute-start.1 = (bf16[128,2304]{1,0:T(8,128)(2,1)S(1)}, bf16[128,2304]{1,0:T(8,128)(2,1)S(1)}, u32[]{:S(2)}, u32[]{:S(2)}) collective-permute-start(bf16[128,2304]{1,0:T(8,128)(2,1)S(1)} %fusion.refs_0_), channel_id=1, source_target_pairs={{0,96},{16,112},{32,0},{48,16},{64,32},{80,48},{96,64},{112,80},{1... | collective-permute-start | bytes 1769480 | tf_op jit(solution)/shard_map/ppermute | solution.py:16
  6.8 14.8 %collective-permute-start = (bf16[128,2304]{1,0:T(8,128)(2,1)S(1)}, bf16[128,2304]{1,0:T(8,128)(2,1)S(1)}, u32[]{:S(2)}, u32[]{:S(2)}) collective-permute-start(bf16[128,2304]{1,0:T(8,128)(2,1)S(1)} %fusion.refs_0_), channel_id=1, source_target_pairs={{0,32},{16,48},{32,64},{48,80},{64,96},{80,112},{96,0},{112,16},{1... | collective-permute-start | bytes 1769480 | tf_op jit(solution)/shard_map/ppermute | solution.py:16
  6.8 7.7 %collective-permute-start.6 = (bf16[64,1152]{1,0:T(8,128)(2,1)S(1)}, bf16[64,1152]{1,0:T(8,128)(2,1)S(1)}, u32[]{:S(2)}, u32[]{:S(2)}) collective-permute-start(bf16[64,1152]{1,0:T(8,128)(2,1)S(1)} %bitcast.12), channel_id=1, source_target_pairs={{0,2},{1,3},{2,4},{3,5},{4,6},{5,7},{6,8},{7,9},{8,10},{9,11},{10,... | collective-permute-start | bytes 442376 | tf_op jit(solution)/shard_map/ppermute | solution.py:30
  14.5 12.9 %collective-permute-start.10 = (bf16[128,1152]{1,0:T(8,128)(2,1)S(1)}, bf16[128,1152]{1,0:T(8,128)(2,1)S(1)}, u32[]{:S(2)}, u32[]{:S(2)}) collective-permute-start(bf16[128,1152]{1,0:T(8,128)(2,1)S(1)} %pad_maximum_fusion.7.refs_9_), channel_id=1, source_target_pairs={{0,12},{1,13},{2,14},{3,15},{4,0},{5,1},{6,2},{7,3},{8,4},{9,5},{1... | collective-permute-start | bytes 884744 | tf_op jit(solution)/shard_map/ppermute | solution.py:30
  14.6 17.6 %collective-permute-start.7 = (bf16[128,1152]{1,0:T(8,128)(2,1)S(1)}, bf16[128,1152]{1,0:T(8,128)(2,1)S(1)}, u32[]{:S(2)}, u32[]{:S(2)}) collective-permute-start(bf16[128,1152]{1,0:T(8,128)(2,1)S(1)} %pad_maximum_fusion.7.refs_9_), channel_id=1, source_target_pairs={{0,4},{1,5},{2,6},{3,7},{4,8},{5,9},{6,10},{7,11},{8,12},{9,13},{1... | collective-permute-start | bytes 884744 | tf_op jit(solution)/shard_map/ppermute | solution.py:30
  21.6 2.2 %slice-start = ((s8[5308416]{0:T(1024)(128)(4,1)}), s8[4194304]{0:T(1024)(128)(4,1)S(1)}, s32[]{:S(2)}) async-start(s8[5308416]{0:T(1024)(128)(4,1)} %bitcast.7), calls=%async_computation | async-start | bytes 8388608
  21.7 2.4 %slice-start.1 = ((s8[5308416]{0:T(1024)(128)(4,1)}), s8[1114112]{0:T(1024)(128)(4,1)S(1)}, s32[]{:S(2)}) async-start(s8[5308416]{0:T(1024)(128)(4,1)} %bitcast.7), calls=%async_computation.1 | async-start | bytes 2228224
  21.9 12.7 %collective-permute-start.5 = (bf16[128,2304]{1,0:T(8,128)(2,1)S(1)}, bf16[128,2304]{1,0:T(8,128)(2,1)S(1)}, u32[]{:S(2)}, u32[]{:S(2)}) collective-permute-start(bf16[128,2304]{1,0:T(8,128)(2,1)S(1)} %get-tuple-element.82), channel_id=1, source_target_pairs={{0,16},{16,0},{32,48},{48,32},{64,80},{80,64},{96,112},{112,96},{1... | collective-permute-start | bytes 1769480 | tf_op jit(solution)/shard_map/ppermute | solution.py:21
  22.1 12.5 %collective-permute-start.4 = (bf16[128,2304]{1,0:T(8,128)(2,1)S(1)}, bf16[128,2304]{1,0:T(8,128)(2,1)S(1)}, u32[]{:S(2)}, u32[]{:S(2)}) collective-permute-start(bf16[128,2304]{1,0:T(8,128)(2,1)S(1)} %get-tuple-element.83), channel_id=1, source_target_pairs={{0,96},{16,112},{32,0},{48,16},{64,32},{80,48},{96,64},{112,80},{1... | collective-permute-start | bytes 1769480 | tf_op jit(solution)/shard_map/ppermute | solution.py:16
  22.4 13.6 %collective-permute-start.3 = (bf16[128,2304]{1,0:T(8,128)(2,1)S(1)}, bf16[128,2304]{1,0:T(8,128)(2,1)S(1)}, u32[]{:S(2)}, u32[]{:S(2)}) collective-permute-start(bf16[128,2304]{1,0:T(8,128)(2,1)S(1)} %get-tuple-element.84), channel_id=1, source_target_pairs={{0,32},{16,48},{32,64},{48,80},{64,96},{80,112},{96,0},{112,16},{1... | collective-permute-start | bytes 1769480 | tf_op jit(solution)/shard_map/ppermute | solution.py:16
  27.4 10.8 %collective-permute-start.11 = (bf16[128,1152]{1,0:T(8,128)(2,1)S(1)}, bf16[128,1152]{1,0:T(8,128)(2,1)S(1)}, u32[]{:S(2)}, u32[]{:S(2)}) collective-permute-start(bf16[128,1152]{1,0:T(8,128)(2,1)S(1)} %collective-permute-done.10.refs_11_), channel_id=1, source_target_pairs={{0,12},{1,13},{2,14},{3,15},{4,0},{5,1},{6,2},{7,3},{8,4},{9,5},{1... | collective-permute-start | bytes 884744 | tf_op jit(solution)/shard_map/ppermute | solution.py:30
  36.3 7.3 %collective-permute-start.9 = (bf16[128,1152]{1,0:T(8,128)(2,1)S(1)}, bf16[128,1152]{1,0:T(8,128)(2,1)S(1)}, u32[]{:S(2)}, u32[]{:S(2)}) collective-permute-start(bf16[128,1152]{1,0:T(8,128)(2,1)S(1)} %pad_maximum_fusion.5), channel_id=1, source_target_pairs={{0,96},{16,112},{32,0},{48,16},{64,32},{80,48},{96,64},{112,80},{1... | collective-permute-start | bytes 884744 | tf_op jit(solution)/shard_map/ppermute | solution.py:16
  36.7 7.0 %collective-permute-start.8 = (bf16[128,1152]{1,0:T(8,128)(2,1)S(1)}, bf16[128,1152]{1,0:T(8,128)(2,1)S(1)}, u32[]{:S(2)}, u32[]{:S(2)}) collective-permute-start(bf16[128,1152]{1,0:T(8,128)(2,1)S(1)} %pad_maximum_fusion.6), channel_id=1, source_target_pairs={{0,32},{16,48},{32,64},{48,80},{64,96},{80,112},{96,0},{112,16},{1... | collective-permute-start | bytes 884744 | tf_op jit(solution)/shard_map/ppermute | solution.py:16
  40.7 13.5 %collective-permute-start.16 = (bf16[128,1152]{1,0:T(8,128)(2,1)S(1)}, bf16[128,1152]{1,0:T(8,128)(2,1)S(1)}, u32[]{:S(2)}, u32[]{:S(2)}) collective-permute-start(bf16[128,1152]{1,0:T(8,128)(2,1)S(1)} %pad_maximum_fusion.7.refs_9_), channel_id=1, source_target_pairs={{0,1},{1,0},{2,3},{3,2},{4,5},{5,4},{6,7},{7,6},{8,9},{9,8},{10,11... | collective-permute-start | bytes 884744 | tf_op jit(solution)/shard_map/ppermute | solution.py:21
  45.9 11.4 %collective-permute-start.15 = (bf16[64,1152]{1,0:T(8,128)(2,1)S(1)}, bf16[64,1152]{1,0:T(8,128)(2,1)S(1)}, u32[]{:S(2)}, u32[]{:S(2)}) collective-permute-start(bf16[64,1152]{1,0:T(8,128)(2,1)S(1)} %get-tuple-element.63), channel_id=1, source_target_pairs={{0,14},{1,15},{2,0},{3,1},{4,2},{5,3},{6,4},{7,5},{8,6},{9,7},{10,... | collective-permute-start | bytes 442376 | tf_op jit(solution)/shard_map/ppermute | solution.py:16
  51.5 5.8 %collective-permute-start.14 = (bf16[64,1152]{1,0:T(8,128)(2,1)S(1)}, bf16[64,1152]{1,0:T(8,128)(2,1)S(1)}, u32[]{:S(2)}, u32[]{:S(2)}) collective-permute-start(bf16[64,1152]{1,0:T(8,128)(2,1)S(1)} %get-tuple-element.64), channel_id=1, source_target_pairs={{0,2},{1,3},{2,4},{3,5},{4,6},{5,7},{6,8},{7,9},{8,10},{9,11},{10,... | collective-permute-start | bytes 442376 | tf_op jit(solution)/shard_map/ppermute | solution.py:16
  51.5 5.8 %collective-permute-start.13 = (bf16[64,1152]{1,0:T(8,128)(2,1)S(1)}, bf16[64,1152]{1,0:T(8,128)(2,1)S(1)}, u32[]{:S(2)}, u32[]{:S(2)}) collective-permute-start(bf16[64,1152]{1,0:T(8,128)(2,1)S(1)} %get-tuple-element.65), channel_id=1, source_target_pairs={{0,14},{1,15},{2,0},{3,1},{4,2},{5,3},{6,4},{7,5},{8,6},{9,7},{10,... | collective-permute-start | bytes 442376 | tf_op jit(solution)/shard_map/ppermute | solution.py:16
  54.2 5.2 %collective-permute-start.12 = (bf16[64,1152]{1,0:T(8,128)(2,1)S(1)}, bf16[64,1152]{1,0:T(8,128)(2,1)S(1)}, u32[]{:S(2)}, u32[]{:S(2)}) collective-permute-start(bf16[64,1152]{1,0:T(8,128)(2,1)S(1)} %get-tuple-element.66), channel_id=1, source_target_pairs={{0,2},{1,3},{2,4},{3,5},{4,6},{5,7},{6,8},{7,9},{8,10},{9,11},{10,... | collective-permute-start | bytes 442376 | tf_op jit(solution)/shard_map/ppermute | solution.py:16
  54.2 14.4 %collective-permute-start.21 = (bf16[256,1152]{1,0:T(8,128)(2,1)S(1)}, bf16[256,1152]{1,0:T(8,128)(2,1)S(1)}, u32[]{:S(2)}, u32[]{:S(2)}) collective-permute-start(bf16[256,1152]{1,0:T(8,128)(2,1)S(1)} %pad_maximum_fusion.4), channel_id=1, source_target_pairs={{0,1},{1,0},{2,3},{3,2},{4,5},{5,4},{6,7},{7,6},{8,9},{9,8},{10,11... | collective-permute-start | bytes 1769480 | tf_op jit(solution)/shard_map/ppermute | solution.py:21
  59.5 4.4 %collective-permute-start.20 = (bf16[64,1152]{1,0:T(8,128)(2,1)S(1)}, bf16[64,1152]{1,0:T(8,128)(2,1)S(1)}, u32[]{:S(2)}, u32[]{:S(2)}) collective-permute-start(bf16[64,1152]{1,0:T(8,128)(2,1)S(1)} %get-tuple-element.61), channel_id=1, source_target_pairs={{0,14},{1,15},{2,0},{3,1},{4,2},{5,3},{6,4},{7,5},{8,6},{9,7},{10,... | collective-permute-start | bytes 442376 | tf_op jit(solution)/shard_map/ppermute | solution.py:16
  60.1 6.9 %collective-permute-start.19 = (bf16[64,1152]{1,0:T(8,128)(2,1)S(1)}, bf16[64,1152]{1,0:T(8,128)(2,1)S(1)}, u32[]{:S(2)}, u32[]{:S(2)}) collective-permute-start(bf16[64,1152]{1,0:T(8,128)(2,1)S(1)} %get-tuple-element.62), channel_id=1, source_target_pairs={{0,2},{1,3},{2,4},{3,5},{4,6},{5,7},{6,8},{7,9},{8,10},{9,11},{10,... | collective-permute-start | bytes 442376 | tf_op jit(solution)/shard_map/ppermute | solution.py:16
  61.0 7.6 %collective-permute-start.17 = (bf16[64,1152]{1,0:T(8,128)(2,1)S(1)}, bf16[64,1152]{1,0:T(8,128)(2,1)S(1)}, u32[]{:S(2)}, u32[]{:S(2)}) collective-permute-start(bf16[64,1152]{1,0:T(8,128)(2,1)S(1)} %fusion.8), channel_id=1, source_target_pairs={{0,2},{1,3},{2,4},{3,5},{4,6},{5,7},{6,8},{7,9},{8,10},{9,11},{10,... | collective-permute-start | bytes 442376 | tf_op jit(solution)/shard_map/ppermute | solution.py:16
  61.2 7.5 %collective-permute-start.18 = (bf16[64,1152]{1,0:T(8,128)(2,1)S(1)}, bf16[64,1152]{1,0:T(8,128)(2,1)S(1)}, u32[]{:S(2)}, u32[]{:S(2)}) collective-permute-start(bf16[64,1152]{1,0:T(8,128)(2,1)S(1)} %fusion.7), channel_id=1, source_target_pairs={{0,14},{1,15},{2,0},{3,1},{4,2},{5,3},{6,4},{7,5},{8,6},{9,7},{10,... | collective-permute-start | bytes 442376 | tf_op jit(solution)/shard_map/ppermute | solution.py:16
  68.7 15.2 %collective-permute-start.27 = (bf16[64,1152]{1,0:T(8,128)(2,1)S(1)}, bf16[64,1152]{1,0:T(8,128)(2,1)S(1)}, u32[]{:S(2)}, u32[]{:S(2)}) collective-permute-start(bf16[64,1152]{1,0:T(8,128)(2,1)S(1)} %fusion.3), channel_id=1, source_target_pairs={{0,2},{1,3},{2,4},{3,5},{4,6},{5,7},{6,8},{7,9},{8,10},{9,11},{10,... | collective-permute-start | bytes 442376 | tf_op jit(solution)/shard_map/ppermute | solution.py:16
  68.8 17.1 %collective-permute-start.29 = (bf16[64,1152]{1,0:T(8,128)(2,1)S(1)}, bf16[64,1152]{1,0:T(8,128)(2,1)S(1)}, u32[]{:S(2)}, u32[]{:S(2)}) collective-permute-start(bf16[64,1152]{1,0:T(8,128)(2,1)S(1)} %fusion.1), channel_id=1, source_target_pairs={{0,14},{1,15},{2,0},{3,1},{4,2},{5,3},{6,4},{7,5},{8,6},{9,7},{10,... | collective-permute-start | bytes 442376 | tf_op jit(solution)/shard_map/ppermute | solution.py:16
  71.5 14.5 %collective-permute-start.23 = (bf16[64,1152]{1,0:T(8,128)(2,1)S(1)}, bf16[64,1152]{1,0:T(8,128)(2,1)S(1)}, u32[]{:S(2)}, u32[]{:S(2)}) collective-permute-start(bf16[64,1152]{1,0:T(8,128)(2,1)S(1)} %get-tuple-element.80), channel_id=1, source_target_pairs={{0,128},{1,129},{2,130},{3,131},{4,132},{5,133},{6,134},{7,135},{8... | collective-permute-start | bytes 442376 | tf_op jit(solution)/shard_map/ppermute | solution.py:39
  80.8 28.5 %collective-permute-start.24 = (bf16[64,1152]{1,0:T(8,128)(2,1)S(1)}, bf16[64,1152]{1,0:T(8,128)(2,1)S(1)}, u32[]{:S(2)}, u32[]{:S(2)}) collective-permute-start(bf16[64,1152]{1,0:T(8,128)(2,1)S(1)} %get-tuple-element.81), channel_id=1, source_target_pairs={{0,129},{1,128},{2,131},{3,130},{4,133},{5,132},{6,135},{7,134},{8... | collective-permute-start | bytes 442376 | tf_op jit(solution)/shard_map/ppermute | solution.py:39
  83.9 13.2 %collective-permute-start.22 = (bf16[128,1152]{1,0:T(8,128)(2,1)S(1)}, bf16[128,1152]{1,0:T(8,128)(2,1)S(1)}, u32[]{:S(2)}, u32[]{:S(2)}) collective-permute-start(bf16[128,1152]{1,0:T(8,128)(2,1)S(1)} %collective-permute-done.11.refs_12_), channel_id=1, source_target_pairs={{0,1},{1,0},{2,3},{3,2},{4,5},{5,4},{6,7},{7,6},{8,9},{9,8},{10,11... | collective-permute-start | bytes 884744 | tf_op jit(solution)/shard_map/ppermute | solution.py:21
  84.0 25.4 %collective-permute-start.25 = (bf16[64,1152]{1,0:T(8,128)(2,1)S(1)}, bf16[64,1152]{1,0:T(8,128)(2,1)S(1)}, u32[]{:S(2)}, u32[]{:S(2)}) collective-permute-start(bf16[64,1152]{1,0:T(8,128)(2,1)S(1)} %get-tuple-element.67), channel_id=1, source_target_pairs={{0,131},{1,130},{2,133},{3,132},{4,135},{5,134},{6,137},{7,136},{8... | collective-permute-start | bytes 442376 | tf_op jit(solution)/shard_map/ppermute | solution.py:39
  85.9 23.4 %collective-permute-start.28 = (bf16[64,1152]{1,0:T(8,128)(2,1)S(1)}, bf16[64,1152]{1,0:T(8,128)(2,1)S(1)}, u32[]{:S(2)}, u32[]{:S(2)}) collective-permute-start(bf16[64,1152]{1,0:T(8,128)(2,1)S(1)} %get-tuple-element.68), channel_id=1, source_target_pairs={{0,130},{1,131},{2,132},{3,133},{4,134},{5,135},{6,136},{7,137},{8... | collective-permute-start | bytes 442376 | tf_op jit(solution)/shard_map/ppermute | solution.py:39
  86.0 23.4 %collective-permute-start.26 = (bf16[64,1152]{1,0:T(8,128)(2,1)S(1)}, bf16[64,1152]{1,0:T(8,128)(2,1)S(1)}, u32[]{:S(2)}, u32[]{:S(2)}) collective-permute-start(bf16[64,1152]{1,0:T(8,128)(2,1)S(1)} %get-tuple-element.69), channel_id=1, source_target_pairs={{0,142},{1,143},{2,128},{3,129},{4,130},{5,131},{6,132},{7,133},{8... | collective-permute-start | bytes 442376 | tf_op jit(solution)/shard_map/ppermute | solution.py:39
  97.1 12.3 %collective-permute-start.30 = (bf16[64,1152]{1,0:T(8,128)(2,1)S(1)}, bf16[64,1152]{1,0:T(8,128)(2,1)S(1)}, u32[]{:S(2)}, u32[]{:S(2)}) collective-permute-start(bf16[64,1152]{1,0:T(8,128)(2,1)S(1)} %get-tuple-element.70), channel_id=1, source_target_pairs={{0,143},{1,142},{2,129},{3,128},{4,131},{5,130},{6,133},{7,132},{8... | collective-permute-start | bytes 442376 | tf_op jit(solution)/shard_map/ppermute | solution.py:39
